TPU v7x, 32 devices: a whole 2x2x4 slice. The times are simulated.
32 devices in a mesh: dp: 16 (over z, y, x), seq: 2 (over core).
Axes of the slice: x: 2, y: 2, z: 4, core: 2. Of those that a mesh axis runs over, the one named last changes fastest.
Arguments:
- tokens_in: bfloat16 [8192, 1536], P(('dp', 'seq')), may hold values from -6 to 6
- cotangent: bfloat16 [8192, 1536], P(('dp', 'seq')), may hold values from -6 to 6
- seq_lens: int32 [16, 4], P('dp'), may hold values from 0 to 512, as said below
- in_weight: float32 [1536, 6448], P(('dp', 'seq')), may hold values from -0.15625 to 0.15625
- in_first: float32 [1536, 6448], P(('dp', 'seq')), may hold values from -32 to 32
- in_second: float32 [1536, 6448], P(('dp', 'seq')), may hold values from 54.0672 to 860.16
- out_weight: float32 [3072, 1536], P(('dp', 'seq')), may hold values from -0.109375 to 0.109375
- out_first: float32 [3072, 1536], P(('dp', 'seq')), may hold values from -56 to 56
- out_second: float32 [3072, 1536], P(('dp', 'seq')), may hold values from 172.032 to 2785.28
- conv_weight: float32 [5, 3328], P(None, ('dp', 'seq')), may hold values from -3 to 3
- conv_first: float32 [5, 3328], P(None, ('dp', 'seq')), may hold values from -32 to 32
- conv_second: float32 [5, 3328], P(None, ('dp', 'seq')), may hold values from 77.824 to 1228.8
- gains: float32 [4608], P(('dp', 'seq')), may hold values from 0.25 to 1.75
- gain_first: float32 [4608], P(('dp', 'seq')), may hold values from -48 to 48
- gain_second: float32 [4608], P(('dp', 'seq')), may hold values from 139.264 to 2211.84
- head_params: float32 [3, 48], replicated, may hold values from -8 to 2.5, as said below
- head_first: float32 [3, 48], replicated, may hold values from -96.302287 to 96.302287, as said below
- head_second: float32 [3, 48], replicated, may hold values from 54.272 to 108926.075, as said below
Outputs:
- mixed_out: bfloat16 [8192, 1536], P(('dp', 'seq'))
- grad_input: float32 [8192, 1536], P(('dp', 'seq'))
- in_weight_new: float32 [1536, 6448], P(('dp', 'seq'))
- in_first_new: float32 [1536, 6448], P(('dp', 'seq'))
- in_second_new: float32 [1536, 6448], P(('dp', 'seq'))
- out_weight_new: float32 [3072, 1536], P(('dp', 'seq'))
- out_first_new: float32 [3072, 1536], P(('dp', 'seq'))
- out_second_new: float32 [3072, 1536], P(('dp', 'seq'))
- conv_weight_new: float32 [5, 3328], P(None, ('dp', 'seq'))
- conv_first_new: float32 [5, 3328], P(None, ('dp', 'seq'))
- conv_second_new: float32 [5, 3328], P(None, ('dp', 'seq'))
- gains_new: float32 [4608], P(('dp', 'seq'))
- gain_first_new: float32 [4608], P(('dp', 'seq'))
- gain_second_new: float32 [4608], P(('dp', 'seq'))
- head_params_new: float32 [3, 48], replicated
- head_first_new: float32 [3, 48], replicated
- head_second_new: float32 [3, 48], replicated
Inputs may be any that keep to these rules, and one draw needn't show every extreme that they name: `seq_lens`: row g lists group g's sequences in order, 0 marking an unused slot. Each takes ceil(length / 256) whole blocks of 256 positions after the earlier ones, all within 512 positions; the first is longer than 256; in some group it fills all 512. `head_params`: row 0 shifts the step sizes, row 1 is the logarithm of the decay rates, row 2 holds positive skip gains. `head_first`: both signs. `head_second`: Positive.
All inputs are finite; a program needn't handle non-finite values.
Results may differ from a plain program's by a relative error of at most 0.012.
Values may be sent and summed in bfloat16 or wider, within the bound.
A program may use at most 256 MiB of HBM per device.

v0:
```python
import functools

import jax
import jax.numpy as jnp
from jax import lax
from jax.experimental import pallas as pl
from jax.experimental.pallas import tpu as pltpu
from jax.sharding import PartitionSpec as P

D = 1536
HEADS = 48
HDIM = 64
NST = 128
KCONV = 4
BLOCK = 256
SLOTS = 4
STEP = 10
DIN = 3072
CONVC = 3328


highest = lax.Precision.HIGHEST
norm_eps = 1e-05
beta_first = 0.9
beta_second = 0.95
adam_eps = 1e-08
weight_decay = 0.1
rate_in = 0.01
rate_out = 0.008
rate_conv = 0.2
rate_gain = 0.4
rate_head = 0.5


def from_behind(block, axis, distance):
    devices = range(lax.axis_size(axis))
    route = [(i - distance, i) for i in devices if i - distance in devices]
    return lax.ppermute(block, axis, route)


def prefix(value, axis, join, neutral):
    place = lax.axis_index(axis)
    gathered = jax.tree.map(
        lambda a, kind: lax.all_gather(a.astype(kind), axis),
        value,
        jax.tree.map(lambda a: jnp.bfloat16 if a.dtype == jnp.float32 else a.dtype, value),
    )
    state = jax.tree.map(lambda a, e: jnp.zeros_like(a) + jnp.asarray(e, a.dtype), value, neutral)

    def one(hop, state):
        return join(
            state,
            jax.tree.map(
                lambda a, own: lax.dynamic_index_in_dim(a, hop, 0, False).astype(own.dtype),
                gathered,
                value,
            ),
        )

    return lax.fori_loop(0, place, one, state)


def prefix_2(value, axis, combine, identity):
    devices, index = (lax.axis_size(axis), lax.axis_index(axis))
    everything = jax.tree.map(
        lambda part, kind: lax.all_gather(part.astype(kind), axis),
        value,
        (jnp.bfloat16, jnp.bfloat16),
    )
    start = jax.tree.map(
        lambda part, zero: jnp.broadcast_to(jnp.asarray(zero, part.dtype), part.shape),
        value,
        identity,
    )

    def hop(k, before):
        at = devices - 1 - k
        reached = at > index
        new = combine(
            before, jax.tree.map(lambda part, own: part[at].astype(own.dtype), everything, value)
        )
        return jax.tree.map(lambda a, b: jnp.where(reached, a, b), new, before)

    return lax.fori_loop(0, devices, hop, start)


def segment_of(seq_row, position):
    blocks = (seq_row + BLOCK - 1) // BLOCK
    ends = jnp.cumsum(blocks) * BLOCK
    starts = ends - blocks * BLOCK
    above = position[:, None] >= starts[None, :]
    inside = above & (position[:, None] < ends[None, :])
    numbers = jnp.arange(1, SLOTS + 1, dtype=jnp.int32)
    labels_of = jnp.sum(jnp.where(inside, numbers[None, :], 0), axis=1)
    live_rows = jnp.sum(
        (above & (position[:, None] < (starts + seq_row)[None, :])).astype(jnp.float32), axis=1
    )
    return (labels_of, live_rows)


def layout(seq_row, position):
    labels_of, live_rows = segment_of(seq_row, position)
    columns = []
    for conv_lag in range(KCONV):
        earlier, unused_live = segment_of(seq_row, position - conv_lag)
        columns.append(((earlier == labels_of) & (labels_of > 0)).astype(jnp.float32))
    return (live_rows, jnp.stack(columns, axis=1))


def pre_norm(token_rows, gain_row):
    scaling = lax.rsqrt(jnp.mean(token_rows * token_rows, axis=1, keepdims=True) + norm_eps)
    return token_rows * scaling * gain_row[None, :]


def gate_norm(mixed, gate_part, gain_row):
    gated = mixed * jax.nn.silu(gate_part)
    scaling = lax.rsqrt(jnp.mean(gated * gated, axis=1, keepdims=True) + norm_eps)
    return gated * scaling * gain_row[None, :]


def mixer_in(extended, step_raw, conv_par, head_values, factors, live_rows):
    row_count = step_raw.shape[0]
    preact = jnp.zeros((row_count, conv_par.shape[1]), jnp.float32) + conv_par[KCONV][None, :]
    for conv_tap in range(KCONV):
        window = lax.slice_in_dim(extended, conv_tap, conv_tap + row_count, axis=0)
        preact = (
            preact
            + conv_par[conv_tap][None, :] * window * factors[:, KCONV - 1 - conv_tap][:, None]
        )
    conv_act = jax.nn.silu(preact)
    step_size = jax.nn.softplus(step_raw + head_values[0][None, :]) * live_rows[:, None]
    logdec = -jnp.exp(head_values[1])[None, :] * step_size
    return (conv_act, step_size, logdec)


def lower_ones():
    row_ids = lax.broadcasted_iota(jnp.int32, (BLOCK, BLOCK), 0)
    col_ids = lax.broadcasted_iota(jnp.int32, (BLOCK, BLOCK), 1)
    return (row_ids >= col_ids).astype(jnp.float32)


def block_state(values, keys_in, step_size, logdec):
    cumul = jnp.dot(lower_ones(), logdec, precision=highest)
    totals = cumul[-1]
    weighting = jnp.exp(totals[None, :] - cumul) * step_size
    states = jnp.einsum("uhp,un->hpn", weighting[:, :, None] * values, keys_in, precision=highest)
    return (jnp.exp(totals), states)


def block_out(values, keys_in, queries, step_size, logdec, skip_gain, start_state):
    lower_tri = lower_ones()
    cumul = jnp.dot(lower_tri, logdec, precision=highest)
    across = cumul.T
    gap_matrix = across[:, :, None] - across[:, None, :]
    decays = jnp.exp(jnp.where(lower_tri[None, :, :] > 0, gap_matrix, -1e30))
    gram_matrix = jnp.dot(queries, keys_in.T, precision=highest)
    mixing = gram_matrix[None, :, :] * decays * step_size.T[:, None, :]
    intra_part = jnp.einsum("htu,uhp->thp", mixing, values, precision=highest)
    carried = jnp.exp(cumul)[:, :, None] * jnp.einsum(
        "tn,hpn->thp", queries, start_state, precision=highest
    )
    return intra_part + carried + skip_gain[None, :, None] * values


def block_full(values, keys_in, queries, step_size, logdec, skip_gain, start_state):
    factor_end, states = block_state(values, keys_in, step_size, logdec)
    outputs = block_out(values, keys_in, queries, step_size, logdec, skip_gain, start_state)
    return (outputs, factor_end[:, None, None] * start_state + states)


def adam_update(weight, first, second, gradient, step_rate):
    first_new = beta_first * first + (1.0 - beta_first) * gradient
    second_new = beta_second * second + (1.0 - beta_second) * gradient * gradient
    first_hat = first_new / (1.0 - beta_first**STEP)
    second_hat = second_new / (1.0 - beta_second**STEP)
    weight_new = weight - step_rate * (
        first_hat / (jnp.sqrt(second_hat) + adam_eps) + weight_decay * weight
    )
    return (weight_new, first_new, second_new)


def carry_join(earlier, later):
    return (earlier[0] * later[0], later[0][:, None, None] * earlier[1] + later[1])


def as_float(array_low):
    return lax.optimization_barrier(array_low).astype(jnp.float32)


def contract_rows(left, right):
    return lax.dot_general(
        left, right, (((0,), (0,)), ((), ())), preferred_element_type=jnp.float32
    )


def contract_cols(left, right):
    return lax.dot_general(
        left, right, (((1,), (1,)), ((), ())), preferred_element_type=jnp.float32
    )


def per_device(
    tokens_in,
    cotangent,
    seq_lens,
    in_weight,
    in_first,
    in_second,
    out_weight,
    out_first,
    out_second,
    conv_weight,
    conv_first,
    conv_second,
    gains,
    gain_first,
    gain_second,
    head_params,
    head_first,
    head_second,
):
    local_tok = tokens_in.shape[0]
    position = lax.axis_index("seq") * local_tok + jnp.arange(local_tok, dtype=jnp.int32)
    live_rows, factors = layout(seq_lens[0], position)
    low_weights = (
        in_weight.astype(jnp.bfloat16),
        out_weight.astype(jnp.bfloat16),
        conv_weight.astype(jnp.bfloat16),
        gains.astype(jnp.bfloat16),
    )
    in_full, out_full, conv_full, gain_full = (
        lax.all_gather(low_weights[0], ("dp", "seq"), axis=0, tiled=True),
        lax.all_gather(low_weights[1], ("dp", "seq"), axis=0, tiled=True),
        lax.all_gather(low_weights[2], ("dp", "seq"), axis=1, tiled=True),
        lax.all_gather(low_weights[3], ("dp", "seq"), axis=0, tiled=True),
    )
    conv_par = conv_full.astype(jnp.float32)
    gain_par = gain_full.astype(jnp.float32)
    token_rows = tokens_in.astype(jnp.float32)
    normed_value, pull_pre = jax.vjp(pre_norm, token_rows, gain_par[:D])
    normed = normed_value.astype(jnp.bfloat16)
    projected = jnp.dot(normed, in_full, preferred_element_type=jnp.float32)
    gate_part = projected[:, :DIN]
    conv_in = projected[:, DIN : DIN + CONVC]
    step_raw = projected[:, DIN + CONVC :]
    halo_rows = from_behind(conv_in[local_tok - KCONV + 1 :], "seq", 1)
    extended = jnp.concatenate([halo_rows, conv_in], axis=0)

    def mixer_local(extended_rows, raw_steps, conv_values, head_values):
        return mixer_in(extended_rows, raw_steps, conv_values, head_values, factors, live_rows)

    (conv_act, step_size, logdec), pull_mixer = jax.vjp(
        mixer_local, extended, step_raw, conv_par, head_params
    )
    conv_used = as_float(conv_act.astype(jnp.bfloat16))
    block_count = local_tok // BLOCK
    values = conv_used[:, :DIN].reshape(block_count, BLOCK, HEADS, HDIM)
    keys_in = conv_used[:, DIN : DIN + NST].reshape(block_count, BLOCK, NST)
    queries = conv_used[:, DIN + NST :].reshape(block_count, BLOCK, NST)
    steps_blk = step_size.reshape(block_count, BLOCK, HEADS)
    logdec_blk = logdec.reshape(block_count, BLOCK, HEADS)
    resets = factors[::BLOCK, 1]
    skip_gain = head_params[2]
    decays, block_states = jax.vmap(block_state)(values, keys_in, steps_blk, logdec_blk)

    def fold_local(carried, block_item):
        factor_now = block_item[0] * block_item[2]
        return (
            (carried[0] * factor_now, factor_now[:, None, None] * carried[1] + block_item[1]),
            None,
        )

    identity = (jnp.ones((HEADS,), jnp.float32), jnp.zeros((HEADS, HDIM, NST), jnp.float32))
    device_sum, unused_fold = lax.scan(fold_local, identity, (decays, block_states, resets))
    unused_dec, entering = prefix(device_sum, "seq", carry_join, identity)

    def start_states(states, block_item):
        begin = block_item[2] * states
        return (block_item[0][:, None, None] * begin + block_item[1], begin)

    unused_end, begins = lax.scan(start_states, entering, (decays, block_states, resets))

    def emit(block_item):
        return block_out(
            block_item[0],
            block_item[1],
            block_item[2],
            block_item[3],
            block_item[4],
            skip_gain,
            block_item[5],
        )

    mixed = lax.map(emit, (values, keys_in, queries, steps_blk, logdec_blk, begins)).reshape(
        local_tok, DIN
    )
    normed_out_value, pull_gate = jax.vjp(gate_norm, mixed, gate_part, gain_par[D:])
    normed_out = normed_out_value.astype(jnp.bfloat16)
    branch = jnp.dot(normed_out, out_full, preferred_element_type=jnp.float32)
    mixed_out = (token_rows + live_rows[:, None] * branch).astype(jnp.bfloat16)
    out_grad = (cotangent.astype(jnp.float32) * live_rows[:, None]).astype(jnp.bfloat16)
    in_back, out_back = (
        lax.all_gather(in_weight.astype(jnp.bfloat16), ("dp", "seq"), axis=0, tiled=True),
        lax.all_gather(out_weight.astype(jnp.bfloat16), ("dp", "seq"), axis=0, tiled=True),
    )
    grad_out_w = contract_rows(normed_out, out_grad)
    grad_normed_out = contract_cols(out_grad, out_back)
    grad_mixed, grad_gate, grad_gain_in = pull_gate(grad_normed_out)
    mixed_back = as_float(grad_mixed.astype(jnp.bfloat16)).reshape(block_count, BLOCK, HEADS, HDIM)

    def adjoint_local(carried, block_item):
        cumul = jnp.dot(lower_ones(), block_item[2], precision=highest)
        weighted = jnp.exp(cumul)[:, :, None] * block_item[0]
        direct = jnp.einsum("thp,tn->hpn", weighted, block_item[1], precision=highest)
        return (block_item[4] * (direct + block_item[3][:, None, None] * carried), None)

    local_adj, unused_adj = lax.scan(
        adjoint_local, identity[1], (mixed_back, queries, logdec_blk, decays, resets), reverse=True
    )
    unused_later, leaving = prefix_2((device_sum[0], local_adj), "seq", carry_join, identity)

    def adjoint_block(carried, block_item):
        unused_primal, pull_block = jax.vjp(
            block_full,
            block_item[0],
            block_item[1],
            block_item[2],
            block_item[3],
            block_item[4],
            skip_gain,
            block_item[5],
        )
        grads = pull_block((block_item[6], carried[0]))
        return ((block_item[7] * grads[6], carried[1] + grads[5]), grads[:5])

    (unused_state, grad_skip), block_grads = lax.scan(
        adjoint_block,
        (leaving, jnp.zeros((HEADS,), jnp.float32)),
        (values, keys_in, queries, steps_blk, logdec_blk, begins, mixed_back, resets),
        reverse=True,
    )
    grad_values, grad_keys, grad_queries, grad_step, grad_logdec = block_grads
    grad_act = jnp.concatenate(
        [
            grad_values.reshape(local_tok, DIN),
            grad_keys.reshape(local_tok, NST),
            grad_queries.reshape(local_tok, NST),
        ],
        axis=1,
    )
    grad_ext, grad_raw, grad_conv, grad_head_part = pull_mixer(
        (grad_act, grad_step.reshape(local_tok, HEADS), grad_logdec.reshape(local_tok, HEADS))
    )
    returned = from_behind(grad_ext[: KCONV - 1].astype(jnp.bfloat16), "seq", -1).astype(
        jnp.float32
    )
    grad_conv_in = grad_ext[KCONV - 1 :] + jnp.concatenate(
        [jnp.zeros((local_tok - KCONV + 1, CONVC), jnp.float32), returned], axis=0
    )
    grad_proj = jnp.concatenate([grad_gate, grad_conv_in, grad_raw], axis=1).astype(jnp.bfloat16)
    grad_normed = contract_cols(grad_proj, in_back)
    grad_rows, grad_gain_pre = pull_pre(grad_normed)
    grad_input = cotangent.astype(jnp.float32) + grad_rows
    grad_gains = jnp.concatenate([grad_gain_pre, grad_gain_in], axis=0)
    grad_head = jnp.concatenate(
        [grad_head_part[:2], (grad_head_part[2] + grad_skip)[None, :]], axis=0
    )
    grad_in_w = contract_rows(normed, grad_proj)
    in_sum, out_sum, conv_sum, gain_sum = (
        lax.psum_scatter(grad_in_w, ("dp", "seq"), scatter_dimension=0, tiled=True),
        lax.psum_scatter(grad_out_w, ("dp", "seq"), scatter_dimension=0, tiled=True),
        lax.psum_scatter(grad_conv, ("dp", "seq"), scatter_dimension=1, tiled=True),
        lax.psum_scatter(grad_gains, ("dp", "seq"), scatter_dimension=0, tiled=True),
    )
    head_sum = lax.psum(grad_head, ("dp", "seq"))
    new_in = adam_update(in_weight, in_first, in_second, in_sum, rate_in)
    new_out = adam_update(out_weight, out_first, out_second, out_sum, rate_out)
    new_conv = adam_update(conv_weight, conv_first, conv_second, conv_sum, rate_conv)
    new_gain = adam_update(gains, gain_first, gain_second, gain_sum, rate_gain)
    new_head = adam_update(head_params, head_first, head_second, head_sum, rate_head)
    return (
        mixed_out,
        grad_input,
        new_in[0],
        new_in[1],
        new_in[2],
        new_out[0],
        new_out[1],
        new_out[2],
        new_conv[0],
        new_conv[1],
        new_conv[2],
        new_gain[0],
        new_gain[1],
        new_gain[2],
        new_head[0],
        new_head[1],
        new_head[2],
    )


MESH_ID = pl.DeviceIdType.MESH
ANY = pl.BlockSpec(memory_space=pl.ANY)
PLANES = 4
QUADS = 4
RANKS = 8


def place():
    chip = lax.axis_index("dp")
    return (chip // QUADS, chip % QUADS, lax.axis_index("seq"))


def at(plane, quad, core):
    return (plane * QUADS + quad, core)


def flip(core):
    return 1 - core


def xor4(value, k):
    low, high = value % 2, value // 2
    if k % 2:
        low = 1 - low
    if k // 2:
        high = 1 - high
    return 2 * high + low


def greet(devices):
    barrier = pltpu.get_barrier_semaphore()
    for device in devices:
        pl.semaphore_signal(barrier, inc=1, device_id=device, device_id_type=MESH_ID)
    pl.semaphore_wait(barrier, len(devices))


def plane_mates(plane, quad, core):
    mates = []
    for k in range(QUADS):
        for other in (core, flip(core)):
            if not (k == 0 and other is core):
                mates.append(at(plane, xor4(quad, k), other))
    return mates


def plane_others(plane, quad, core):
    return [at(xor4(plane, k), quad, core) for k in range(1, PLANES)]


class Sems:
    def __init__(self, send, recv):
        self.send, self.recv, self.used = (send, recv, 0)

    def copy(self, source, target, device):
        index = self.used
        self.used += 1
        return pltpu.make_async_remote_copy(
            src_ref=source,
            dst_ref=target,
            send_sem=self.send.at[index],
            recv_sem=self.recv.at[index],
            device_id=device,
            device_id_type=MESH_ID,
        )


class PlaneGather:
    def __init__(self, sems, own, land, plane, quad, core):
        near_x, near_y, far = (xor4(quad, k) for k in (1, 2, 3))
        rank, rank_x, rank_y, rank_far = (2 * q + core for q in (quad, near_x, near_y, far))
        to_x, to_y = (at(plane, near_x, core), at(plane, near_y, core))
        sibling = at(plane, quad, flip(core))
        whole = [0, 1]
        self.own = [
            sems.copy(own(h), land(rank, slot, h), device)
            for device, slot in ((to_x, 1), (to_y, 2), (sibling, 0))
            for h in whole
        ]
        self.relay_x = [
            sems.copy(land(rank_x, 1, 0), land(rank_x, 3, 0), to_y),
        ] + [sems.copy(land(rank_x, 1, h), land(rank_x, 1, h), sibling) for h in whole]
        self.relay_y = [
            sems.copy(land(rank_y, 2, 1), land(rank_y, 3, 1), to_x),
        ] + [sems.copy(land(rank_y, 2, h), land(rank_y, 2, h), sibling) for h in whole]
        self.relay_far = [
            sems.copy(land(rank_far, 3, h), land(rank_far, 3, h), sibling) for h in whole
        ]

    def start(self):
        for copy in self.own:
            copy.start()

    def near(self):
        self.own[0].wait_recv()
        self.relay_x[0].start()
        self.own[3].wait_recv()
        self.relay_y[0].start()
        self.own[1].wait_recv()
        self.own[2].wait_recv()
        for copy in self.relay_x[1:] + self.relay_y[1:]:
            copy.start()

    def across(self):
        for h, relay in ((0, self.relay_x[0]), (1, self.relay_y[0])):
            relay.wait_recv()
            self.relay_far[h].start()

    def wait_slot(self, slot):
        for copy in (self.own[4:], self.relay_x[1:], self.relay_y[1:], self.relay_far)[slot]:
            copy.wait_recv()

    def sent(self):
        for copy in self.own + self.relay_x + self.relay_y + self.relay_far:
            copy.wait_send()


class LineGather:
    def __init__(self, sems, own, block, plane, quad, core):
        self.plane = plane
        self.right, self.left = ([], [])
        for hop in range(PLANES - 1):
            for copies, step in ((self.right, 1), (self.left, -1)):
                index = plane - step * hop
                source = own if hop == 0 else block(index)
                copies.append(sems.copy(source, block(index), at(plane + step, quad, core)))

    def sends(self, hop, step):
        if step > 0:
            return (self.plane - hop >= 0) & (self.plane < PLANES - 1)
        return (self.plane + hop < PLANES) & (self.plane > 0)

    def receives(self, hop, step):
        if step > 0:
            return self.plane - 1 - hop >= 0
        return self.plane + 1 + hop < PLANES

    def start(self, hop):
        for copies, step in ((self.right, 1), (self.left, -1)):

            @pl.when(self.sends(hop, step))
            def go():
                copies[hop].start()

    def arrive(self, hop):
        for copies, step in ((self.right, 1), (self.left, -1)):

            @pl.when(self.receives(hop, step))
            def landed():
                copies[hop].wait_recv()

    def sent(self):
        for hop in range(PLANES - 1):
            for copies, step in ((self.right, 1), (self.left, -1)):

                @pl.when(self.sends(hop, step))
                def left():
                    copies[hop].wait_send()


OWN_HEADS = HEADS // RANKS
OWN = OWN_HEADS * HDIM
PAIRS = OWN_HEADS // 2
RUN = OWN // 2
COMMON = 2 * NST + HEADS
COMMON_PAD = 384
GROUP = 2 * BLOCK
MIX = OWN + 2 * NST
LANES = 128
STRIP = 128


def mm(left, right):
    return lax.dot_general(left, right, (((1,), (0,)), ((), ())), preferred_element_type=jnp.float32)


def mm_t(left, right):
    return lax.dot_general(left, right, (((1,), (1,)), ((), ())), preferred_element_type=jnp.float32)


def t_mm(left, right):
    return lax.dot_general(left, right, (((0,), (0,)), ((), ())), preferred_element_type=jnp.float32)


def mm_full(left, right):
    return lax.dot_general(
        left, right, (((1,), (0,)), ((), ())), precision=highest, preferred_element_type=jnp.float32
    )


def low16(value):
    return value.astype(jnp.bfloat16)


def parts_of(value, terms):
    parts = []
    for unused in range(terms):
        parts.append(low16(value))
        value = value - parts[-1].astype(jnp.float32)
    return parts


def mm_right(left, ones, terms=3):
    return sum(mm(part, ones) for part in parts_of(left, terms))


def mm_left(ones, right, terms=3):
    return sum(mm(ones, part) for part in parts_of(right, terms))


def iota(shape, axis):
    return lax.broadcasted_iota(jnp.int32, shape, axis)


def head_spread():
    return low16((iota((LANES, OWN), 1) // HDIM == iota((LANES, OWN), 0)).astype(jnp.float32))


def head_gather():
    return low16((iota((OWN, LANES), 0) // HDIM == iota((OWN, LANES), 1)).astype(jnp.float32))


def lower_mask():
    return iota((BLOCK, BLOCK), 0) >= iota((BLOCK, BLOCK), 1)


def shift_down(value, k):
    if k == 0:
        return value
    rolled = pltpu.roll(value, k, 0)
    return jnp.where(iota(value.shape, 0) >= k, rolled, 0.0)


def shift_up(value, k):
    if k == 0:
        return value
    rows = value.shape[0]
    rolled = pltpu.roll(value, rows - k, 0)
    return jnp.where(iota(value.shape, 0) < rows - k, rolled, 0.0)


def sigmoid(value):
    return 1.0 / (1.0 + jnp.exp(-value))


def softplus(value):
    return jnp.maximum(value, 0.0) + jnp.log1p(jnp.exp(-jnp.abs(value)))


def preact_of(u, conv):
    total = u * conv[KCONV - 1 : KCONV] + conv[KCONV : KCONV + 1]
    for tap in range(KCONV - 1):
        total = total + shift_down(u, KCONV - 1 - tap) * conv[tap : tap + 1]
    return total


def steps_of(raw, heads, live):
    step = softplus(raw + heads[0:1]) * live * heads[3:4]
    return (step, -jnp.exp(heads[1:2]) * step)


def lane_half(value, side):
    lanes = iota(value.shape, 1)
    return jnp.where((lanes >= HDIM) == (side == 1), value, jnp.zeros_like(value))


def block_parts(step, logdec, spread):
    cumul = mm_left(low16(lower_mask().astype(jnp.float32)), logdec)
    return (cumul, jnp.transpose(cumul), mm_right(step, spread, 2), mm_right(cumul, spread))


def ssd_forward(act, step, logdec, skip, out):
    spread = head_spread()
    lower = lower_mask()
    state = None
    for k in range(2):
        rows = slice(k * BLOCK, (k + 1) * BLOCK)
        values, keys, queries = (act[rows, :OWN], act[rows, OWN : OWN + NST], act[rows, OWN + NST :])
        cumul, cumul_t, step_w, cumul_w = block_parts(step[rows], logdec[rows], spread)
        gram = jnp.where(lower, mm_t(queries, keys), 0.0)
        values_f = values.astype(jnp.float32)
        stepped = low16(values_f * step_w)
        base = skip * values_f
        if state is not None:
            base = base + jnp.exp(cumul_w) * mm(queries, state)
        else:
            weighting = jnp.exp(cumul_w[BLOCK - 1 :] - cumul_w) * step_w
            state = low16(t_mm(keys, low16(weighting * values_f)))

        for pair in range(PAIRS):
            lanes = slice(pair * LANES, (pair + 1) * LANES)
            sides = [lane_half(stepped[:, lanes], side) for side in range(2)]
            for start in range(0, BLOCK, STRIP):
                strip, wide = (slice(start, start + STRIP), start + STRIP)
                piece = base[strip, lanes]
                for side in range(2):
                    h = 2 * pair + side
                    decay = jnp.exp(jnp.minimum(cumul[strip, h : h + 1] - cumul_t[h : h + 1, :wide], 0.0))
                    piece = piece + mm(low16(gram[strip, :wide] * decay), sides[side][:wide])
                out[k * BLOCK + start : k * BLOCK + wide, lanes] = piece


def live_of(lens, g):
    rows = iota((GROUP, 1), 0).astype(jnp.float32)
    chosen = jnp.sum(jnp.where(iota(lens.shape, 0) == g, lens, 0.0), axis=0, keepdims=True)[:, :1]
    return (rows < chosen).astype(jnp.float32)


def quad_of(slot):
    quad = lax.axis_index("dp") % QUADS
    return (quad % 2 + slot % 2) % 2 + 2 * ((quad // 2 + slot // 2) % 2)


def full_spec(shape):
    return pl.BlockSpec(shape, lambda g: (0,) * len(shape))


def group_spec(width):
    return pl.BlockSpec((GROUP, width), lambda g: (g, 0))


VMEM_GRANT = 60 * 1024 * 1024


def backward_block(k, act, dmix, step, logdec, skip, state, state_grad, spread, gather):
    rows = slice(k * BLOCK, (k + 1) * BLOCK)
    values, keys, queries = (act[rows, :OWN], act[rows, OWN : OWN + NST], act[rows, OWN + NST :])
    step, logdec = (step[rows], logdec[rows])
    lower = lower_mask()
    cumul, cumul_t, step_w, cumul_w = block_parts(step, logdec, spread)
    step_t = jnp.transpose(step)
    gram = jnp.where(lower, mm_t(queries, keys), 0.0)
    values_f = values.astype(jnp.float32)
    dmix_f = dmix[rows].astype(jnp.float32)
    lanes_h = iota((BLOCK, LANES), 1)

    rows_h = iota((8, BLOCK), 0)
    strips = [slice(i * STRIP, (i + 1) * STRIP) for i in range(BLOCK // STRIP)]
    widths = [-(-strip.stop // LANES) * LANES for strip in strips]
    grams = [gram[strip, :wide] for strip, wide in zip(strips, widths)]
    grad_grams = [0.0] * len(strips)
    row_sums = [jnp.zeros((STRIP, LANES), jnp.float32)] * len(strips)
    lanes_h = iota((STRIP, LANES), 1)
    col_sums = jnp.zeros((8, BLOCK), jnp.float32)
    pieces = []
    for pair in range(PAIRS):
        lanes = slice(pair * LANES, (pair + 1) * LANES)
        dm, value = (dmix[rows, lanes], act[rows, lanes])
        piece = [0.0] * (BLOCK // LANES)
        for side in range(2):
            h = 2 * pair + side
            dm_half = lane_half(dm, side)
            sums = [0.0] * (BLOCK // LANES)
            for i, (strip, wide) in enumerate(zip(strips, widths)):
                decay = jnp.exp(jnp.minimum(cumul[strip, h : h + 1] - cumul_t[h : h + 1, :wide], 0.0))
                grad_mixing = mm_t(dm_half[strip], value[:wide])
                mixing = grams[i] * decay
                step_row = step_t[h : h + 1, :wide]
                grad_grams[i] = grad_grams[i] + grad_mixing * decay * step_row
                product = grad_mixing * mixing
                row_sums[i] = jnp.where(
                    lanes_h == h, jnp.sum(product * step_row, axis=1, keepdims=True), row_sums[i]
                )
                column = jnp.sum(product, axis=0, keepdims=True)
                part = t_mm(low16(mixing), dm_half[strip])
                for c in range(wide // LANES):
                    own = slice(c * LANES, (c + 1) * LANES)
                    sums[c] = sums[c] + column[:, own]
                    piece[c] = piece[c] + part[own]
            col_sums = jnp.where(rows_h == h, jnp.concatenate(sums, axis=1), col_sums)
        pieces.append(jnp.concatenate(piece, axis=0))
    row_sums = jnp.concatenate(row_sums, axis=0)
    grad_values = jnp.concatenate(pieces, axis=1) * step_w + skip * dmix_f
    grad_skip = jnp.sum(dmix_f * values_f, axis=0, keepdims=True)
    grad_queries, grad_keys = ([], [0.0] * (BLOCK // LANES))
    for strip, wide, grad_gram in zip(strips, widths, grad_grams):
        kept = low16(jnp.where(lower[strip, :wide], grad_gram, 0.0))
        grad_queries.append(mm(kept, keys[:wide]))
        part = t_mm(kept, queries[strip])
        for c in range(wide // LANES):
            grad_keys[c] = grad_keys[c] + part[c * LANES : (c + 1) * LANES]
    grad_queries = jnp.concatenate(grad_queries, axis=0)
    grad_keys = jnp.concatenate(grad_keys, axis=0)
    columns = jnp.transpose(
        jnp.concatenate([col_sums, jnp.zeros((LANES - 8, BLOCK), jnp.float32)], axis=0)
    )
    grad_step = columns
    grad_cumul = row_sums - columns * step
    if k == 1:
        entering = jnp.exp(cumul_w) * dmix_f
        entering_low = low16(entering)
        crossed = mm(queries, state)
        grad_cumul = grad_cumul + mm_right(entering * crossed, gather, 2)
        grad_queries = grad_queries + mm_t(entering_low, state)
        before = low16(t_mm(queries, entering_low))
    else:
        tail = jnp.exp(cumul_w[BLOCK - 1 :] - cumul_w)
        weighting = tail * step_w
        back = mm(keys, state_grad)
        grad_values = grad_values + weighting * back
        grad_keys = grad_keys + mm_t(low16(weighting * values_f), state_grad)
        grad_weight = mm_right(values_f * back, gather, 2)
        tail_h = jnp.exp(cumul[BLOCK - 1 :] - cumul)
        grad_step = grad_step + grad_weight * tail_h
        part = grad_weight * tail_h * step
        last = iota((BLOCK, LANES), 0) == BLOCK - 1
        grad_cumul = grad_cumul - part + jnp.where(last, jnp.sum(part, axis=0, keepdims=True), 0.0)
        before = None
    upper = low16((iota((BLOCK, BLOCK), 0) <= iota((BLOCK, BLOCK), 1)).astype(jnp.float32))
    grad_logdec = mm_left(upper, grad_cumul)
    return (grad_values, grad_keys, grad_queries, grad_step, grad_logdec, grad_skip, before)


ROWS_IN = D // (PLANES * RANKS)
ROWS_OUT = DIN // (PLANES * RANKS)
ROWS_ALL = ROWS_IN + 16
SHARD_CONV = CONVC // (PLANES * RANKS)
SHARD_GAIN = (D + DIN) // (PLANES * RANKS)
RUN_HALVES = RUN // HDIM


def place_lanes(pieces, tiles, rows):
    lanes = iota((rows, LANES), 1)
    out = [jnp.zeros((rows, LANES), jnp.float32) for unused in range(tiles)]
    for value, width, offset in pieces:
        tile, lane = divmod(offset, LANES)
        moved = pltpu.roll(value, lane, 1) if lane else value
        end = lane + width
        out[tile] = jnp.where((lanes >= lane) & (lanes < end), moved, out[tile])
        if end > LANES:
            out[tile + 1] = jnp.where(lanes < end - LANES, moved, out[tile + 1])
    return out


def own_lanes(tiles, quad, core):
    rows = tiles[0].shape[0]
    lanes = iota((rows, LANES), 1)

    def half_of(index):
        tile, odd = (index // 2, index % 2)
        chosen = tiles[0]
        for t in range(1, len(tiles)):
            chosen = jnp.where(tile == t, tiles[t], chosen)
        return (chosen, odd)

    out = []
    for pair in range(PAIRS):
        sides = []
        for b in range(2):
            near, i = divmod(2 * pair + b, RUN_HALVES)
            value, odd = half_of(2 * PLANES * RUN_HALVES * core + PLANES * RUN_HALVES * near + RUN_HALVES * quad + i)
            sides.append(jnp.where(odd == b, value, pltpu.roll(value, HDIM, 1)))
        out.append(jnp.where(lanes < HDIM, sides[0], sides[1]))
    return jnp.concatenate(out, axis=1)


def fill_sends(in_w, part, target):
    lanes = iota((ROWS_IN, LANES), 1)
    for j in range(RANKS):
        quad, core = divmod(j, 2)
        for pair in range(PAIRS):
            sides = []
            for b in range(2):
                near, i = divmod(2 * pair + b, RUN_HALVES)
                index = (2 * core + near) * PLANES * RUN_HALVES + RUN_HALVES * quad + i
                start = part * DIN + index // 2 * LANES
                tile = in_w[:, start : start + LANES]
                sides.append(tile if index % 2 == b else pltpu.roll(tile, HDIM, 1))
            lane = pair * LANES
            target[j, :, lane : lane + LANES] = low16(jnp.where(lanes < HDIM, sides[0], sides[1]))


def fill_common(in_w, conv_w, gains, lens, wc_send):
    wc_send[...] = jnp.zeros_like(wc_send)
    wc_send[:ROWS_IN, : 2 * NST] = low16(in_w[:, 2 * DIN : 2 * DIN + 2 * NST])
    tail = in_w[:, 2 * DIN + 2 * NST : 2 * DIN + COMMON]
    wide = jnp.concatenate([tail, jnp.zeros((ROWS_IN, LANES - HEADS), jnp.float32)], axis=1)
    wc_send[:ROWS_IN, 2 * NST :] = low16(wide)
    conv_v = jnp.concatenate([conv_w[...], jnp.zeros((KCONV + 1, COMMON_PAD - SHARD_CONV), jnp.float32)], axis=1)
    gain_v = jnp.concatenate([gains[...], jnp.zeros((1, COMMON_PAD - SHARD_GAIN), jnp.float32)], axis=1)
    extra = jnp.broadcast_to(lens[:, 0:1].astype(jnp.float32) - BLOCK, (1, COMMON_PAD))
    rows = jnp.concatenate([conv_v, gain_v, extra, jnp.zeros((9, COMMON_PAD), jnp.float32)], axis=0)
    wc_send[ROWS_IN:] = low16(rows)


def select_heads(quad, core):
    rows, columns = (iota((LANES, LANES), 0), iota((LANES, LANES), 1))
    head = HEADS // 2 * core + HEADS // 4 * (columns // 3) + 3 * quad + columns % 3
    return ((rows == head) & (columns < OWN_HEADS)).astype(jnp.float32)


def fore_kernel(
    tok, cot, seq_lens, in_w, out_w, conv_w, gains, head_params,
    o_normed, o_cot, o_gate_w, o_x_w, o_com, o_out, o_gate, o_proj, o_proj_com, o_act, o_mixed, o_gno,
    stats, gain_in, gain_out, conv, heads, skip, select, lens,
    wx_send, wg_send, wc_send, wo_send, all_tok, all_cot, normed, all_wx, all_wg, all_wc, w_com, line_wo, w_out,
    proj, gate, proj_com, act, mixed, gno, part, shared,
    send, recv, local
):
    plane, quad, core = place()
    where = (plane, quad, core)
    rank = 2 * quad + core
    sibling = at(plane, quad, flip(core))
    sems = Sems(send, recv)
    f32 = jnp.float32
    half = BLOCK // 2
    kept = []

    def keep(source, target):
        copy = pltpu.make_async_copy(source, target, local.at[len(kept)])
        kept.append(copy)
        copy.start()
        return copy

    def pieces(buffer):
        return lambda r, slot, h: buffer.at[slot, core, pl.ds(h * half, half)]

    def halves(buffer):
        return lambda h: buffer.at[pl.ds(h * half, half)]

    push_c = [
        sems.copy(wc_send, all_wc.at[plane, rank], at(xor4(plane, k), quad, core)) for k in (2, 3, 1)
    ]
    line_o = LineGather(sems, wo_send, lambda q: line_wo.at[q], *where)
    line_x = LineGather(sems, all_wx.at[plane], lambda q: all_wx.at[q], *where)
    line_g = LineGather(sems, all_wg.at[plane], lambda q: all_wg.at[q], *where)
    shuffles = []
    for source, target in ((wx_send, all_wx), (wg_send, all_wg)):
        copies = []
        for k in range(1, RANKS):
            other_core = flip(core) if k % 2 else core
            other_quad = xor4(quad, k // 2)
            copies.append(
                sems.copy(
                    source.at[2 * other_quad + other_core], target.at[plane, rank], at(plane, other_quad, other_core)
                )
            )
        shuffles.append(copies)
    tokens = PlaneGather(sems, halves(tok), pieces(all_tok), *where)
    grads = PlaneGather(sems, halves(cot), pieces(all_cot), *where)
    common = PlaneGather(
        sems,
        lambda h: all_wc.at[pl.ds(2 * h, 2), rank],
        lambda r, slot, h: all_wc.at[pl.ds(2 * h, 2), r],
        *where,
    )
    cross_o = [
        sems.copy(line_wo.at[2 * flip(core) + k], w_out.at[k, core], sibling) for k in range(2)
    ]
    mates = plane_mates(*where)
    swap = [sems.copy(part, shared.at[rank], device) for device in mates]

    greet(mates + plane_others(*where))
    fill_common(in_w, conv_w, gains, seq_lens, wc_send)
    for copy in push_c:
        copy.start()
    fill_sends(in_w, 1, wx_send)
    for copy in shuffles[0]:
        copy.start()
    wo_send[...] = low16(out_w[...])
    line_o.start(0)
    fill_sends(in_w, 0, wg_send)
    for copy in shuffles[1]:
        copy.start()
    own_wx = keep(wx_send.at[rank], all_wx.at[plane, rank])
    own_wg = keep(wg_send.at[rank], all_wg.at[plane, rank])
    own_wc = keep(wc_send, all_wc.at[plane, rank])
    own_tok = keep(tok, all_tok.at[0, core])
    own_cot = keep(cot, all_cot.at[0, core])
    own_wo = keep(wo_send, line_wo.at[plane])
    own_wc.wait()
    for copy in push_c:
        copy.wait_recv()
    common.start()
    own_wx.wait()
    for copy in shuffles[0]:
        copy.wait_recv()
    line_x.start(0)
    tokens.start()
    select[...] = select_heads(quad, core)
    wide = jnp.concatenate([head_params[...], jnp.zeros((3, LANES - HEADS), f32)], axis=1)
    wide = jnp.concatenate([wide, jnp.ones((1, LANES), f32), jnp.zeros((4, LANES), f32)], axis=0)
    heads[...] = mm_full(wide * (iota((8, LANES), 1) < HEADS).astype(f32), select[...])
    skip[...] = mm_right(heads[2:3], head_spread())

    common.near()
    common.across()
    for slot in range(QUADS):
        common.wait_slot(slot)
    line_x.arrive(0)
    line_x.start(1)
    for q in range(PLANES):
        for r in range(RANKS):
            start = (RANKS * q + r) * ROWS_IN
            w_com[start : start + ROWS_IN] = all_wc[q, r, :ROWS_IN]
    keep(w_com, o_com)
    extras = [all_wc[q, r, ROWS_IN:].astype(f32) for q in range(PLANES) for r in range(RANKS)]
    gain_tiles = place_lanes(
        [(e[5:6, :LANES], LANES, SHARD_GAIN * d) for d, e in enumerate(extras)]
        + [(e[5:6, LANES : 2 * LANES], SHARD_GAIN - LANES, SHARD_GAIN * d + LANES) for d, e in enumerate(extras)],
        (D + DIN) // LANES,
        1,
    )
    gain_in[...] = jnp.concatenate(gain_tiles[: D // LANES], axis=1)
    gain_out[...] = own_lanes(gain_tiles[D // LANES :], quad, core)
    conv_tiles = place_lanes(
        [(e[:8, :LANES], SHARD_CONV, SHARD_CONV * d) for d, e in enumerate(extras)], CONVC // LANES, 8
    )
    conv[...] = jnp.concatenate(
        [own_lanes(conv_tiles[: DIN // LANES], quad, core)] + conv_tiles[DIN // LANES :], axis=1
    )
    seats = []
    for slot in range(QUADS):
        chosen = jnp.zeros((1, LANES), f32)
        for q in range(PLANES):
            for p in range(QUADS):
                here = (plane == q) & (quad_of(slot) == p)
                chosen = jnp.where(here, extras[RANKS * q + 2 * p][6:7, :LANES], chosen)
        seats.append(chosen + BLOCK)
    lens[...] = jnp.concatenate(seats + [jnp.zeros((8 - QUADS, LANES), f32)], axis=0)

    def norm(slot):
        for side in range(2):
            rows = all_tok[slot, side].astype(f32)
            scaling = lax.rsqrt(jnp.mean(rows * rows, axis=1, keepdims=True) + norm_eps)
            normed[slot, pl.ds(side * BLOCK, BLOCK)] = low16(rows * scaling * gain_in[...])

    own_tok.wait()
    tokens.wait_slot(0)
    norm(0)
    line_x.arrive(1)
    line_x.start(2)
    own_wg.wait()
    for copy in shuffles[1]:
        copy.wait_recv()
    line_g.start(0)
    tokens.near()
    grads.start()
    line_x.arrive(2)
    keep(all_wx, o_x_w)

    @pl.loop(0, QUADS)
    def each(slot):
        @pl.when(slot == 1)
        def first():
            tokens.wait_slot(1)
            norm(1)
            line_g.arrive(0)
            line_g.start(1)

        @pl.when(slot == 2)
        def second():
            tokens.wait_slot(2)
            norm(2)
            tokens.across()
            line_g.arrive(1)
            line_g.start(2)

        @pl.when(slot == 3)
        def third():
            tokens.wait_slot(3)
            norm(3)
            line_o.arrive(0)
            line_o.start(1)

        proj[slot] = mm(normed[slot], all_wx[...].reshape(D, OWN))
        proj_com[slot] = mm(normed[slot], w_com[...])
        conv_in = jnp.concatenate([proj[slot], proj_com[slot, :, : 2 * NST]], axis=1)
        raw = mm_right(proj_com[slot, :, 2 * NST :], low16(select[...]))
        preact = preact_of(conv_in, conv[...])
        act[slot] = low16(preact * sigmoid(preact))
        step, logdec = steps_of(raw, heads[...], live_of(lens[...], slot))
        ssd_forward(act.at[slot], step, logdec, skip[...], mixed.at[slot])

    for slot in range(QUADS):
        keep(normed.at[slot], o_normed.at[pl.ds(slot * GROUP, GROUP)])
    for source, target in ((proj, o_proj), (proj_com, o_proj_com), (act, o_act), (mixed, o_mixed)):
        keep(source, target)
    line_g.arrive(2)
    line_o.arrive(1)
    line_o.start(2)
    keep(all_wg, o_gate_w)
    grads.near()

    @pl.loop(0, QUADS)
    def gates(slot):
        gate[slot] = mm(normed[slot], all_wg[...].reshape(D, OWN))

    keep(gate, o_gate)
    line_o.arrive(2)
    own_wo.wait()
    for copy in cross_o:
        copy.start()
    for k in range(2):
        w_out[k, core] = line_wo[2 * core + k]
    own_cot.wait()
    for copy in cross_o:
        copy.wait_recv()
    keep(w_out, o_out)
    part[...] = jnp.zeros_like(part)

    @pl.loop(0, QUADS)
    def measure(slot):
        for k in range(QUADS):

            @pl.when(slot == k)
            def here():
                if k == 1:
                    grads.across()
                grads.wait_slot(k)

        live = live_of(lens[...], slot)
        grad = all_cot[slot].reshape(GROUP, D)
        grad = jnp.where(live > 0.0, grad, jnp.zeros_like(grad))
        gno_v = mm_t(grad, w_out[...].reshape(OWN, D))
        gno[slot] = gno_v
        gate_part = gate[slot]
        gated = mixed[slot] * gate_part * sigmoid(gate_part)
        squares = jnp.sum(gated * gated, axis=1, keepdims=True)
        inner = jnp.sum(gno_v * gain_out[...] * gated, axis=1, keepdims=True)
        lanes = iota((GROUP, LANES), 1)
        seat = quad_of(slot)
        columns = jnp.where(lanes == 2 * seat, squares, 0.0) + jnp.where(lanes == 2 * seat + 1, inner, 0.0)
        part[...] += jnp.transpose(columns)[:8]

    for copy in swap:
        copy.start()
    keep(all_cot, o_cot)
    keep(gno, o_gno)
    shared[rank] = part[...]
    for copy in swap:
        copy.wait_recv()
    stats[...] = jnp.sum(shared[...], axis=0)
    for copy in shuffles[0] + shuffles[1] + push_c + cross_o + swap:
        copy.wait_send()
    for line in (line_o, line_x, line_g):
        line.sent()
    for gather in (tokens, grads, common):
        gather.sent()
    for copy in kept:
        if not any(copy is done for done in (own_wx, own_wg, own_wc, own_tok, own_cot, own_wo)):
            copy.wait()


def run_fore(tok, cot, seq_lens, in_w, out_w, conv_w, gains, head_params):
    f32, bf16 = (jnp.float32, jnp.bfloat16)
    whole = pl.BlockSpec(memory_space=pltpu.VMEM)
    outs = (
        ((QUADS * GROUP, D), bf16), ((QUADS, 2, BLOCK, D), bf16), ((PLANES, RANKS, ROWS_IN, OWN), bf16),
        ((PLANES, RANKS, ROWS_IN, OWN), bf16), ((D, COMMON_PAD), bf16), ((2, 2, ROWS_OUT, D), bf16),
        ((QUADS, GROUP, OWN), f32), ((QUADS, GROUP, OWN), f32), ((QUADS, GROUP, COMMON_PAD), f32), ((QUADS, GROUP, MIX), bf16),
        ((QUADS, GROUP, OWN), f32), ((QUADS, GROUP, OWN), f32),
    )
    small = (
        (8, GROUP), (1, D), (1, OWN), (8, MIX), (8, LANES), (1, OWN), (LANES, LANES), (8, LANES),
    )
    scratch = (
        ((RANKS, ROWS_IN, OWN), bf16), ((RANKS, ROWS_IN, OWN), bf16), ((ROWS_ALL, COMMON_PAD), bf16), ((ROWS_OUT, D), bf16),
        ((QUADS, 2, BLOCK, D), bf16), ((QUADS, 2, BLOCK, D), bf16), ((QUADS, GROUP, D), bf16),
        ((PLANES, RANKS, ROWS_IN, OWN), bf16), ((PLANES, RANKS, ROWS_IN, OWN), bf16),
        ((PLANES, RANKS, ROWS_ALL, COMMON_PAD), bf16),
        ((D, COMMON_PAD), bf16), ((PLANES, ROWS_OUT, D), bf16), ((2, 2, ROWS_OUT, D), bf16),
        ((QUADS, GROUP, OWN), f32), ((QUADS, GROUP, OWN), f32), ((QUADS, GROUP, COMMON_PAD), f32),
        ((QUADS, GROUP, MIX), bf16), ((QUADS, GROUP, OWN), f32), ((QUADS, GROUP, OWN), f32), ((8, GROUP), f32),
        ((RANKS, 8, GROUP), f32),
    )
    args = (tok, cot, seq_lens, in_w, out_w, conv_w, gains.reshape(1, -1), head_params)
    results = pl.pallas_call(
        fore_kernel,
        in_specs=[ANY, ANY] + [whole] * 6,
        out_specs=[ANY] * len(outs) + [whole] * len(small),
        out_shape=[jax.ShapeDtypeStruct(s, kind) for s, kind in outs]
        + [jax.ShapeDtypeStruct(s, f32) for s in small],
        scratch_shapes=[pltpu.VMEM(s, kind) for s, kind in scratch]
        + [
            pltpu.SemaphoreType.DMA((96,)),
            pltpu.SemaphoreType.DMA((96,)),
            pltpu.SemaphoreType.DMA((24,)),
        ],
        compiler_params=pltpu.CompilerParams(
            vmem_limit_bytes=VMEM_GRANT, collective_id=0, has_side_effects=True
        ),
    )(*args)
    rows = QUADS * GROUP
    widths = (D, D, None, None, None, None, OWN, OWN, COMMON_PAD, MIX, OWN, OWN)
    flat = [a if w is None else a.reshape(rows, w) for a, w in zip(results, widths)]
    flat[2], flat[3] = (flat[2].reshape(D, OWN), flat[3].reshape(D, OWN))
    flat[5] = flat[5].reshape(OWN, D)
    return flat + list(results[len(outs) :])


def gate_kernel(
    lens, stats, cot, normed, gate_part, mixed, grad_normed_out, w_out, gain_out,
    branch, dgate, dmix, g_out, g_gate, g_gain, acc_out, acc_gate, tmp_out_t, tmp_grad
):
    g = pl.program_id(0)
    live = live_of(lens[...], g)

    @pl.when(g == 0)
    def first():
        acc_out[...] = jnp.zeros_like(acc_out)
        acc_gate[...] = jnp.zeros_like(acc_gate)
        g_gain[...] = jnp.zeros_like(g_gain)

    columns = jnp.transpose(jnp.concatenate([stats[...], jnp.zeros((LANES - 8, GROUP), jnp.float32)], axis=0))
    lanes = iota((GROUP, LANES), 1)
    seat = quad_of(g)
    power = jnp.sum(jnp.where(lanes == 2 * seat, columns, 0.0), axis=1, keepdims=True)
    along = jnp.sum(jnp.where(lanes == 2 * seat + 1, columns, 0.0), axis=1, keepdims=True)
    scale_out = lax.rsqrt(power * (1.0 / DIN) + norm_eps)
    gate_v, mixed_v, gno = (gate_part[...], mixed[...], grad_normed_out[...])
    sig = sigmoid(gate_v)
    gate_act = gate_v * sig
    gated = mixed_v * gate_act
    normed_out = low16(gated * scale_out * gain_out[...])
    tmp_out_t[...] = jnp.transpose(normed_out)
    tmp_grad[...] = jnp.where(live > 0.0, cot[...], jnp.zeros_like(cot[...]))
    scaled = gno * scale_out
    grad_gated = scaled * gain_out[...] - gated * (scale_out * scale_out * scale_out * along * (1.0 / DIN))
    gain_sum = jnp.sum(scaled * gated, axis=0, keepdims=True)
    g_gain[...] += jnp.concatenate([gain_sum, jnp.zeros((7, OWN), jnp.float32)], axis=0)
    grad_gate = low16(grad_gated * mixed_v * (sig * (1.0 + gate_v * (1.0 - sig))))
    dgate[...] = grad_gate
    dmix[...] = low16(grad_gated * gate_act)
    wide = 4 * LANES
    for side in range(2):
        branch[0, side] = low16(mm(normed_out[side * BLOCK : (side + 1) * BLOCK], w_out[...]))

    @pl.loop(0, D // wide)
    def tile(i):
        lanes = pl.ds(pl.multiple_of(i * wide, wide), wide)
        acc_out[:, lanes] += mm(tmp_out_t[...], tmp_grad[:, lanes])
        acc_gate[lanes, :] += t_mm(normed[:, lanes], dgate[...])

    @pl.when(g == QUADS - 1)
    def last():
        g_out[...] = low16(acc_out[...])
        g_gate[...] = low16(acc_gate[...])


def run_gate(lens, stats, cot, normed, gate_part, mixed, grad_normed_out, w_out, gain_out):
    f32, bf16 = (jnp.float32, jnp.bfloat16)
    rows = QUADS * GROUP
    grouped = (cot, normed, gate_part, mixed, grad_normed_out)
    ends = (((OWN, D), bf16), ((D, OWN), bf16), ((8, OWN), f32))
    return pl.pallas_call(
        gate_kernel,
        grid=(QUADS,),
        in_specs=[full_spec(a.shape) for a in (lens, stats)]
        + [group_spec(a.shape[1]) for a in grouped]
        + [full_spec(w_out.shape), full_spec(gain_out.shape)],
        out_specs=[pl.BlockSpec((1, 2, BLOCK, D), lambda g: (g, 0, 0, 0)), group_spec(OWN), group_spec(OWN)]
        + [full_spec(s) for s, kind in ends],
        out_shape=[
            jax.ShapeDtypeStruct((QUADS, 2, BLOCK, D), bf16),
            jax.ShapeDtypeStruct((rows, OWN), bf16),
            jax.ShapeDtypeStruct((rows, OWN), bf16),
        ]
        + [jax.ShapeDtypeStruct(s, kind) for s, kind in ends],
        scratch_shapes=[
            pltpu.VMEM((OWN, D), f32), pltpu.VMEM((D, OWN), f32),
            pltpu.VMEM((OWN, GROUP), bf16), pltpu.VMEM((GROUP, D), bf16),
        ],
        compiler_params=pltpu.CompilerParams(vmem_limit_bytes=VMEM_GRANT),
    )(lens, stats, *grouped, w_out, gain_out)


def backward_group(live, dmix, conv_in, raw, act, conv, heads, skip, between):
    raw_v = raw[...]
    heads_v = heads[...]
    step, logdec = steps_of(raw_v, heads_v, live)
    spread, gather = (head_spread(), head_gather())
    rows0 = slice(0, BLOCK)
    cumul0 = mm_left(low16(lower_mask().astype(jnp.float32)), logdec[rows0])
    cumul0_w = mm_right(cumul0, spread)
    weighting = jnp.exp(cumul0_w[BLOCK - 1 :] - cumul0_w) * mm_right(step[rows0], spread, 2)
    state = low16(
        t_mm(act[rows0, OWN : OWN + NST], low16(weighting * act[rows0, :OWN].astype(jnp.float32)))
    )
    late = backward_block(1, act, dmix, step, logdec, skip[...], state, None, spread, gather)
    between()
    early = backward_block(0, act, dmix, step, logdec, skip[...], None, late[6], spread, gather)
    grad_act = jnp.concatenate([jnp.concatenate(part[:3], axis=1) for part in (early, late)], axis=0)
    grad_step = jnp.concatenate([early[3], late[3]], axis=0)
    grad_logdec = jnp.concatenate([early[4], late[4]], axis=0)
    rate = jnp.exp(heads_v[1:2])
    grad_raw = (grad_step - rate * grad_logdec) * live * heads_v[3:4] * sigmoid(raw_v + heads_v[0:1])
    u = conv_in[...]
    conv_v = conv[...]
    preact = preact_of(u, conv_v)
    sig_q = sigmoid(preact)
    grad_pre = grad_act * (sig_q * (1.0 + preact * (1.0 - sig_q)))
    grad_u = grad_pre * conv_v[KCONV - 1 : KCONV]
    taps = []
    for tap in range(KCONV):
        lag = KCONV - 1 - tap
        if lag:
            grad_u = grad_u + shift_up(grad_pre, lag) * conv_v[tap : tap + 1]
        taps.append(jnp.sum(grad_pre * shift_down(u, lag), axis=0, keepdims=True))
    taps.append(jnp.sum(grad_pre, axis=0, keepdims=True))
    small = (
        jnp.concatenate(taps + [jnp.zeros((3, MIX), jnp.float32)], axis=0),
        jnp.sum(grad_raw, axis=0, keepdims=True),
        jnp.sum(grad_logdec * logdec, axis=0, keepdims=True),
        early[5] + late[5],
    )
    return (grad_u, grad_raw, small)


PACK = 48


def back_kernel(
    lens, gate_grads, out_grads, branch_all, w_gate, w_x, w_com, conv, heads, skip, select, gain_in, g_gain,
    tok_own, normed, dgate, dmix, proj_x, proj_com, act,
    r_out, all_gate, all_x, sum_com, packs, sum_branch, grad_rows,
    acc_x, acc_com, small_conv, small_head, small_skip,
    branch_own, branch_sib, en_part, en_sib, branch_got, en_got, branch_relay, en_relay,
    gate_got, gate_own, sum_gate, x_send, x_got, x_passed, sum_x, com_send, com_sib, com_quad, com_z, com_got,
    pack_send, pack_got, pack_sum,
    sends, recvs, out_send, out_recv, local
):
    s = pl.program_id(0)
    slot = QUADS - 1 - s
    plane, quad, core = place()
    where = (plane, quad, core)
    rank = 2 * quad + core
    sibling = at(plane, quad, flip(core))
    f32 = jnp.float32
    sems = Sems(sends, recvs)
    to_x, to_y = (at(plane, xor4(quad, 1), core), at(plane, xor4(quad, 2), core))
    half = BLOCK // 2

    swaps = [
        [sems.copy(branch_all.at[k, flip(core)], branch_sib.at[k], sibling) for k in range(QUADS)],
        [sems.copy(en_part.at[k % 2, flip(core)], en_sib.at[k], sibling) for k in range(QUADS)],
    ]
    routes = []
    for sib, got, relay in ((branch_sib, branch_got, branch_relay), (en_sib, en_got, en_relay)):
        routes.append(
            {
                "relay_x": sems.copy(sib.at[3, pl.ds(0, half)], relay.at[0], to_x),
                "relay_y": sems.copy(sib.at[3, pl.ds(half, half)], relay.at[1], to_y),
                "x": sems.copy(sib.at[1], got.at[0], to_x),
                "y": sems.copy(sib.at[2], got.at[1], to_y),
            }
        )

    def z_push(source, target):
        return [
            sems.copy(source.at[xor4(plane, k)], target.at[k - 1], at(xor4(plane, k), quad, core))
            for k in (2, 3, 1)
        ]

    def rank_push(source, target):
        copies = []
        for k in range(1, RANKS):
            other_core = flip(core) if k % 2 else core
            other_quad = xor4(quad, k // 2)
            copies.append(
                sems.copy(source(2 * other_quad + other_core), target.at[rank], at(plane, other_quad, other_core))
            )
        return copies

    gate_z = z_push(gate_grads, gate_got)
    x_z = z_push(x_send, x_got)
    x_relay = sems.copy(x_send.at[xor4(plane, 3)], x_passed, at(xor4(plane, 1), quad, core))
    at_end = plane % (PLANES - 1) == 0
    part_rows = D // PLANES
    gate_ranks = rank_push(lambda r: sum_gate.at[r], all_gate)
    x_ranks = rank_push(lambda r: sum_x.at[r], all_x)
    com_swap = sems.copy(com_send.at[:, :, flip(core)], com_sib, sibling)
    com_quads = [
        sems.copy(com_sib.at[:, xor4(quad, k)], com_quad.at[k - 1], at(plane, xor4(quad, k), core))
        for k in (3, 1, 2)
    ]
    com_planes = z_push(com_z, com_got)
    pack_z = [
        sems.copy(pack_send, pack_got.at[k - 1], at(xor4(plane, k), quad, core)) for k in (2, 3, 1)
    ]
    pack_ranks = rank_push(lambda r: pack_sum, packs)

    def out_copy(near, side):
        return pltpu.make_async_remote_copy(
            src_ref=out_grads.at[near, side],
            dst_ref=r_out.at[plane],
            send_sem=out_send.at[2 * near + side],
            recv_sem=out_recv.at[plane],
            device_id=at(2 * core + near, quad, side),
            device_id_type=MESH_ID,
        )

    def out_landing(origin):
        return pltpu.make_async_remote_copy(
            src_ref=out_grads.at[0, 0],
            dst_ref=r_out.at[origin],
            send_sem=out_send.at[0],
            recv_sem=out_recv.at[origin],
            device_id=sibling,
            device_id_type=MESH_ID,
        )

    out_here = pltpu.make_async_copy(out_grads.at[plane % 2, core], r_out.at[plane], local.at[0])
    out_stays = plane // 2 == core
    gate_here = pltpu.make_async_copy(gate_grads.at[plane], gate_own, local.at[1])
    branch_here = [
        pltpu.make_async_copy(branch_all.at[k, core], branch_own.at[k], local.at[5 + k]) for k in range(QUADS)
    ]

    @pl.when(s == 0)
    def begin():
        peers = plane_mates(*where) + plane_others(*where)
        peers += [at(xor4(plane, k), quad, flip(core)) for k in range(1, PLANES)]
        greet(peers)
        for copy in gate_z:
            copy.start()
        for copy in swaps[0][::-1]:
            copy.start()
        for near in range(2):
            for side in range(2):

                @pl.when(jnp.logical_not((2 * core + near == plane) & (core == side)))
                def go():
                    out_copy(near, side).start()

        @pl.when(out_stays)
        def stay():
            out_here.start()

        for copy in branch_here[::-1]:
            copy.start()
        gate_here.start()
        for ref in (acc_x, acc_com, small_conv, small_head, small_skip):
            ref[...] = jnp.zeros_like(ref)

    def settle(kind, k, own, sib):
        route = routes[kind]
        relay = (branch_relay, en_relay)[kind]
        swaps[kind][k].wait_recv()
        sib[k] = low16(own.astype(f32) + sib[k].astype(f32))
        if k == 3:
            route["relay_x"].start()
            route["relay_y"].start()
        if k == 2:
            route["relay_x"].wait_recv()
            sib[k, :half] = low16(sib[k, :half].astype(f32) + relay[0].astype(f32))
            route["y"].start()
        if k == 1:
            route["relay_y"].wait_recv()
            sib[k, half:] = low16(sib[k, half:].astype(f32) + relay[1].astype(f32))
            route["x"].start()

    def settle_branch(k):
        branch_here[k].wait()
        settle(0, k, branch_own[k], branch_sib)

    def between():
        for k in range(QUADS):

            @pl.when(slot == k)
            def sums():
                if k < QUADS - 1:
                    settle(1, k + 1, en_part[(k + 1) % 2, core], en_sib)
                if k == 3:
                    settle_branch(3)
                if k == 2:
                    settle_branch(1)

    live = live_of(lens[...], slot)
    conv_in = jnp.concatenate([proj_x[...], proj_com[:, : 2 * NST]], axis=1)
    raw = mm_right(proj_com[:, 2 * NST :], low16(select[...]))
    grad_u, grad_raw, small = backward_group(
        live, dmix, conv_in, raw, act, conv, heads, skip, between
    )
    small_conv[...] += small[0]
    small_head[0:1] += small[1]
    small_head[1:2] += small[2]
    small_skip[0:1] += small[3]
    raw_wide = mm_t(low16(grad_raw), low16(select[...]))
    grad_x = low16(grad_u[:, :OWN])
    grad_com = low16(jnp.concatenate([grad_u[:, OWN:], raw_wide], axis=1))
    normed_v = normed[...]
    acc_x[...] += t_mm(normed_v, grad_x)

    @pl.when(s == QUADS - 1)
    def send_x():
        x_send[...] = low16(acc_x[...]).reshape(x_send.shape)

        @pl.when(at_end)
        def from_end():
            x_relay.start()

        @pl.when(jnp.logical_not(at_end))
        def from_middle():
            x_z[1].start()
            x_z[2].start()

    acc_com[...] += t_mm(normed_v, grad_com)

    @pl.when(s == QUADS - 1)
    def send_com():
        com_send[...] = low16(acc_com[...]).reshape(com_send.shape)
        com_swap.start()

    for k in range(2):

        @pl.when(slot == k)
        def free():
            swaps[1][k + 2].wait_send()

    for side in range(2):
        rows = slice(side * BLOCK, (side + 1) * BLOCK)
        en_part[slot % 2, side] = low16(
            mm_t(dgate[rows], w_gate[...]) + mm_t(grad_x[rows], w_x[...]) + mm_t(grad_com[rows], w_com[...])
        )
    for k in range(QUADS):

        @pl.when(slot == k)
        def swap_en():
            swaps[1][k].start()

    for k, done in ((3, 2), (2, 0)):

        @pl.when(slot == k)
        def settle_late():
            settle_branch(done)

    @pl.when(s == QUADS - 1)
    def tail():
        @pl.when(at_end)
        def rest_from_end():
            x_relay.wait_send()
            x_z[0].start()
            x_z[2].start()

        @pl.when(jnp.logical_not(at_end))
        def pass_on():
            x_relay.wait_recv()
            far = xor4(plane, 2)
            x_send[far] = low16(x_send[far].astype(f32) + x_passed[...].astype(f32))
            x_z[0].start()

        settle(1, 0, en_part[0, core], en_sib)
        gate_here.wait()
        for copy in gate_z:
            copy.wait_recv()
        sum_gate[...] = low16(
            gate_own[...].astype(f32) + gate_got[0].astype(f32) + gate_got[1].astype(f32) + gate_got[2].astype(f32)
        )
        for copy in gate_ranks:
            copy.start()
        gate_keep = pltpu.make_async_copy(sum_gate.at[rank], all_gate.at[rank], local.at[2])
        gate_keep.start()
        com_swap.wait_recv()
        com_sib[...] = low16(com_sib[...].astype(f32) + com_send[:, :, core].astype(f32))
        for copy in com_quads:
            copy.start()
        for name in ("x", "y"):
            routes[0][name].wait_recv()
        sum_branch[...] = (
            branch_sib[0].astype(f32) + branch_got[0].astype(f32) + branch_got[1].astype(f32)
        )
        for copy in com_quads:
            copy.wait_recv()
        com_z[...] = low16(
            com_sib[:, quad].astype(f32)
            + com_quad[0].astype(f32) + com_quad[1].astype(f32) + com_quad[2].astype(f32)
        )
        for copy in com_planes:
            copy.start()
        for name in ("x", "y"):
            routes[1][name].wait_recv()
        en = en_sib[0].astype(f32) + en_got[0].astype(f32) + en_got[1].astype(f32)
        rows = tok_own[...].astype(f32)
        scaling = lax.rsqrt(jnp.mean(rows * rows, axis=1, keepdims=True) + norm_eps)
        scaled = rows * scaling
        gain_grad = jnp.sum(en * scaled, axis=0, keepdims=True)
        weighted = en * gain_in[...]
        inner = jnp.mean(weighted * scaled, axis=1, keepdims=True)
        grad_rows[...] = scaling * (weighted - scaled * inner)
        pack_send[...] = jnp.zeros_like(pack_send)
        for i in range(D // LANES):
            pack_send[i : i + 1] = gain_grad[:, i * LANES : (i + 1) * LANES]
        gain_out_grad = g_gain[0:1]
        skip_grad = small_skip[0:1]
        for i in range(PAIRS):
            lanes = slice(i * LANES, (i + 1) * LANES)
            pack_send[12 + i : 13 + i] = gain_out_grad[:, lanes]
            pack_send[42 + i : 43 + i] = skip_grad[:, lanes]
            for tap in range(KCONV + 1):
                pack_send[15 + 3 * tap + i : 16 + 3 * tap + i] = small_conv[tap : tap + 1, lanes]
        for tap in range(KCONV + 1):
            for i in range(2):
                lanes = slice(OWN + i * LANES, OWN + (i + 1) * LANES)
                pack_send[30 + 2 * tap + i : 31 + 2 * tap + i] = small_conv[tap : tap + 1, lanes]
        pack_send[40:42] = small_head[0:2]
        for copy in pack_z:
            copy.start()
        for copy in com_planes:
            copy.wait_recv()
        sum_com[...] = (
            com_z[plane].astype(f32)
            + com_got[0].astype(f32) + com_got[1].astype(f32) + com_got[2].astype(f32)
        )
        for copy in pack_z:
            copy.wait_recv()
        pack_sum[...] = pack_send[...] + pack_got[0] + pack_got[1] + pack_got[2]
        for copy in pack_ranks:
            copy.start()
        pack_keep = pltpu.make_async_copy(pack_sum, packs.at[rank], local.at[3])
        pack_keep.start()
        x_z[0].wait_recv()
        x_z[2].wait_recv()
        acc_x[:part_rows] = (
            x_send[plane].astype(f32) + x_got[0].astype(f32) + x_got[1].astype(f32)
        ).reshape(part_rows, OWN)

        @pl.when(jnp.logical_not(at_end))
        def one_more():
            x_z[1].wait_recv()
            acc_x[:part_rows] += x_got[2].astype(f32).reshape(part_rows, OWN)

        sum_x[...] = low16(acc_x[:part_rows]).reshape(sum_x.shape)
        for copy in x_ranks:
            copy.start()
        x_keep = pltpu.make_async_copy(sum_x.at[rank], all_x.at[rank], local.at[4])
        x_keep.start()
        for origin in range(PLANES):

            @pl.when(jnp.logical_not((plane == origin) & out_stays))
            def arrived():
                out_landing(origin).wait_recv()

        @pl.when(out_stays)
        def kept():
            out_here.wait()

        for near in range(2):
            for side in range(2):

                @pl.when(jnp.logical_not((2 * core + near == plane) & (core == side)))
                def gone():
                    out_copy(near, side).wait_send()

        for copy in gate_ranks + pack_ranks + x_ranks:
            copy.wait_recv()
        @pl.when(jnp.logical_not(at_end))
        def middle_sent():
            x_z[1].wait_send()

        for copy in gate_z + [x_z[0], x_z[2]] + gate_ranks + x_ranks + [com_swap] + com_quads + com_planes + pack_z + pack_ranks:
            copy.wait_send()
        for copy in swaps[0] + swaps[1][:2] + list(routes[0].values()) + list(routes[1].values()):
            copy.wait_send()
        gate_keep.wait()
        pack_keep.wait()
        x_keep.wait()


def run_back(lens, gate_grads, out_grads, branch, w_gate, w_x, w_com, conv, heads, skip, select, gain_in, g_gain, tok_own,
             normed, dgate, dmix, proj_x, proj_com, act):
    f32, bf16 = (jnp.float32, jnp.bfloat16)
    rows_in = D // (PLANES * RANKS)
    rows_out = DIN // (PLANES * RANKS)
    gate_grads = gate_grads.reshape(PLANES, RANKS, rows_in, OWN)
    out_grads = out_grads.reshape(2, 2, rows_out, D)
    fixed = (w_gate, w_x, w_com, conv, heads, skip, select, gain_in, g_gain, tok_own)
    grouped = (normed, dgate, dmix, proj_x, proj_com, act)

    def turned(width):
        return pl.BlockSpec((GROUP, width), lambda s: (QUADS - 1 - s, 0))

    outs = (
        ((PLANES, rows_out, D), bf16, ANY),
        ((RANKS, rows_in, OWN), bf16, ANY),
        ((RANKS, rows_in, OWN), bf16, ANY),
        ((rows_in, COMMON_PAD), f32, None),
        ((RANKS, PACK, LANES), f32, ANY),
        ((BLOCK, D), f32, None),
        ((BLOCK, D), f32, None),
    )
    half = BLOCK // 2
    quarter = (RANKS, rows_in, OWN)
    com = (rows_in, COMMON_PAD)
    scratch = [
        ((D, OWN), f32), ((D, COMMON_PAD), f32), ((8, MIX), f32), ((8, LANES), f32), ((8, OWN), f32),
        ((QUADS, BLOCK, D), bf16),
        ((QUADS, BLOCK, D), bf16), ((2, 2, BLOCK, D), bf16), ((QUADS, BLOCK, D), bf16),
        ((2, BLOCK, D), bf16), ((2, BLOCK, D), bf16), ((2, half, D), bf16), ((2, half, D), bf16),
        ((PLANES - 1,) + quarter, bf16), (quarter, bf16), (quarter, bf16),
        ((PLANES,) + quarter, bf16), ((PLANES - 1,) + quarter, bf16), (quarter, bf16), (quarter, bf16),
        ((PLANES, QUADS, 2) + com, bf16), ((PLANES, QUADS) + com, bf16), ((QUADS - 1, PLANES) + com, bf16),
        ((PLANES,) + com, bf16), ((PLANES - 1,) + com, bf16),
        ((PACK, LANES), f32), ((PLANES - 1, PACK, LANES), f32), ((PACK, LANES), f32),
    ]
    return pl.pallas_call(
        back_kernel,
        grid=(QUADS,),
        in_specs=[full_spec(lens.shape), ANY, ANY, ANY]
        + [full_spec(a.shape) for a in fixed]
        + [turned(a.shape[1]) for a in grouped],
        out_specs=[full_spec(s) if spec is None else spec for s, kind, spec in outs],
        out_shape=[jax.ShapeDtypeStruct(s, kind) for s, kind, spec in outs],
        scratch_shapes=[pltpu.VMEM(s, kind) for s, kind in scratch]
        + [
            pltpu.SemaphoreType.DMA((64,)),
            pltpu.SemaphoreType.DMA((64,)),
            pltpu.SemaphoreType.DMA((4,)),
            pltpu.SemaphoreType.DMA((4,)),
            pltpu.SemaphoreType.DMA((9,)),
        ],
        compiler_params=pltpu.CompilerParams(
            vmem_limit_bytes=VMEM_GRANT, collective_id=2, has_side_effects=True
        ),
    )(lens, gate_grads, out_grads, branch, *fixed, *grouped)


def adam_refs(refs, index, gradient, rate):
    weight, first, second, weight_new, first_new, second_new = refs
    results = adam_update(weight[index], first[index], second[index], gradient, rate)
    for ref, value in zip((weight_new, first_new, second_new), results):
        ref[index] = value


def finish_kernel(
    lens, tok, cot, sum_branch, grad_rows, r_out, all_gate, all_x, sum_com,
    in_w, in_m, in_v, out_w, out_m, out_v,
    mixed_out, grad_input, in_wn, in_mn, in_vn, out_wn, out_mn, out_vn
):
    f32 = jnp.float32
    core = lax.axis_index("seq")
    position = (iota((BLOCK, 1), 0) + core * BLOCK).astype(f32)
    live = (position < lens[0:1, 0:1]).astype(f32)
    mixed_out[...] = (tok[...].astype(f32) + live * sum_branch[...]).astype(jnp.bfloat16)
    grad_input[...] = cot[...].astype(f32) + grad_rows[...]
    ins = (in_w, in_m, in_v, in_wn, in_mn, in_vn)
    rows = in_w.shape[0]
    lanes = iota((rows, LANES), 1)
    for part, source in ((0, all_gate), (1, all_x)):
        for run in range(PLANES):
            side, near = divmod(run, 2)
            tiles = []
            for t in range(2 * PAIRS):
                halves = []
                for b in range(2):
                    p, i = divmod(2 * t + b, 3)
                    index = 3 * near + i
                    tile = source[2 * p + side, :, (index // 2) * LANES : (index // 2 + 1) * LANES].astype(f32)
                    halves.append(tile if index % 2 == b else pltpu.roll(tile, HDIM, 1))
                tiles.append(jnp.where(lanes < HDIM, halves[0], halves[1]))
            start = part * DIN + run * 2 * OWN
            adam_refs(ins, (slice(None), slice(start, start + 2 * OWN)), jnp.concatenate(tiles, axis=1), rate_in)
    adam_refs(ins, (slice(None), slice(2 * DIN, 2 * DIN + COMMON)), sum_com[:, :COMMON], rate_in)
    total = r_out[0].astype(f32) + r_out[1].astype(f32) + r_out[2].astype(f32) + r_out[3].astype(f32)
    adam_refs((out_w, out_m, out_v, out_wn, out_mn, out_vn), (slice(None), slice(None)), total, rate_out)


def run_finish(*args):
    tok, cot, in_w, out_w = (args[1], args[2], args[9], args[12])
    shapes = [(tok.shape, jnp.bfloat16), (cot.shape, jnp.float32)]
    shapes += [(in_w.shape, jnp.float32)] * 3 + [(out_w.shape, jnp.float32)] * 3
    whole = pl.BlockSpec(memory_space=pltpu.VMEM)
    return pl.pallas_call(
        finish_kernel,
        in_specs=[whole] * len(args),
        out_specs=[whole] * len(shapes),
        out_shape=[jax.ShapeDtypeStruct(s, kind) for s, kind in shapes],
        compiler_params=pltpu.CompilerParams(vmem_limit_bytes=VMEM_GRANT),
    )(*args)


def pick_runs(array, plane_runs, quad, core):
    lead = array.shape[:-1]
    width = array.shape[-1] // (PLANES * QUADS)
    split = array.reshape(lead + (2, 2, QUADS, width))
    zero = 0
    n = len(lead)
    taken = lax.dynamic_slice(
        split, (zero,) * n + (core, 0, quad, 0), lead + (1, 2, 1, width)
    )
    return taken.reshape(lead + (2 * width,))


def put_runs(array, quad, core):
    lead = array.shape[:-1]
    width = array.shape[-1] // 2
    zeros = jnp.zeros(lead + (2, 2, QUADS, width), array.dtype)
    n = len(lead)
    full = lax.dynamic_update_slice(
        zeros, array.reshape(lead + (1, 2, 1, width)), (0,) * n + (core, 0, quad, 0)
    )
    return full.reshape(lead + (width * PLANES * QUADS,))


def rank_slices(array):
    rows = array.shape[0]
    split = array.reshape(rows, 2, 2, QUADS, RUN)
    return split.transpose(3, 1, 0, 2, 4).reshape(RANKS, rows, OWN)


def rank_join(array):
    rows = array.shape[1]
    split = array.reshape(QUADS, 2, rows, 2, RUN)
    return split.transpose(2, 1, 3, 0, 4).reshape(rows, DIN)


def per_device_quad(
    tokens_in,
    cotangent,
    seq_lens,
    in_weight,
    in_first,
    in_second,
    out_weight,
    out_first,
    out_second,
    conv_weight,
    conv_first,
    conv_second,
    gains,
    gain_first,
    gain_second,
    head_params,
    head_first,
    head_second,
):
    plane, quad, core = place()
    rank = 2 * quad + core
    (
        normed, cot, w_gate, w_x, w_com, w_out, gate_part, proj_x, proj_com, act, mixed, grad_normed_out,
        stats, gain_in, gain_out, conv, heads, skip, select, lens
    ) = run_fore(tokens_in, cotangent, seq_lens, in_weight, out_weight, conv_weight, gains, head_params)
    branch, dgate, dmix, g_out, g_gate, g_gain = run_gate(
        lens, stats, cot, normed, gate_part, mixed, grad_normed_out, w_out, gain_out
    )
    r_out, all_gate, all_x, sum_com, packs, sum_branch, grad_rows = run_back(
        lens, g_gate, g_out, branch, w_gate, w_x, w_com, conv, heads, skip, select, gain_in, g_gain,
        tokens_in, normed, dgate, dmix, proj_x, proj_com, act
    )
    finished = run_finish(
        lens, tokens_in, cotangent, sum_branch, grad_rows, r_out, all_gate, all_x, sum_com,
        in_weight, in_first, in_second, out_weight, out_first, out_second
    )
    mine = rank + RANKS * plane
    grad_gains = jnp.concatenate(
        [jnp.sum(packs[:, :12], axis=0).reshape(D), rank_join(packs[:, 12:15].reshape(RANKS, 1, OWN)).reshape(DIN)]
    )
    gain_sum = lax.dynamic_slice(grad_gains, (mine * gains.shape[0],), gains.shape)
    grad_conv = jnp.concatenate(
        [
            rank_join(packs[:, 15:30].reshape(RANKS, KCONV + 1, OWN)),
            jnp.sum(packs[:, 30:40], axis=0).reshape(KCONV + 1, 2 * NST),
        ],
        axis=1,
    )
    conv_sum = lax.dynamic_slice(grad_conv, (0, mine * conv_weight.shape[1]), conv_weight.shape)
    grad_skip = jnp.sum(packs[:, 42:45].reshape(RANKS, 1, OWN_HEADS, HDIM), axis=3)
    head_sum = jnp.concatenate([packs[:, 40:42, :OWN_HEADS], grad_skip], axis=1)
    head_sum = head_sum.reshape(QUADS, 2, 3, 2, 3).transpose(2, 1, 3, 0, 4).reshape(3, HEADS)
    new_conv = adam_update(conv_weight, conv_first, conv_second, conv_sum, rate_conv)
    new_gain = adam_update(gains, gain_first, gain_second, gain_sum, rate_gain)
    new_head = adam_update(head_params, head_first, head_second, head_sum, rate_head)
    return tuple(finished) + new_conv + new_gain + new_head


def solution(mesh):
    placed = (
        P(("dp", "seq"), None),
        P(("dp", "seq"), None),
        P("dp", None),
        P(("dp", "seq"), None),
        P(("dp", "seq"), None),
        P(("dp", "seq"), None),
        P(("dp", "seq"), None),
        P(("dp", "seq"), None),
        P(("dp", "seq"), None),
        P(None, ("dp", "seq")),
        P(None, ("dp", "seq")),
        P(None, ("dp", "seq")),
        P(("dp", "seq")),
        P(("dp", "seq")),
        P(("dp", "seq")),
        P(),
        P(),
        P(),
    )
    quad = dict(mesh.shape) == {"dp": PLANES * QUADS, "seq": 2}
    return jax.shard_map(
        per_device_quad if quad else per_device,
        mesh=mesh,
        in_specs=placed,
        out_specs=(
            P(("dp", "seq"), None),
            P(("dp", "seq"), None),
            P(("dp", "seq"), None),
            P(("dp", "seq"), None),
            P(("dp", "seq"), None),
            P(("dp", "seq"), None),
            P(("dp", "seq"), None),
            P(("dp", "seq"), None),
            P(None, ("dp", "seq")),
            P(None, ("dp", "seq")),
            P(None, ("dp", "seq")),
            P(("dp", "seq")),
            P(("dp", "seq")),
            P(("dp", "seq")),
            P(),
            P(),
            P(),
        ),
        check_vma=False,
    )
```

profile of v0, /device:TPU:0, one launch (start us, length us, event | category | flops | bytes accessed | tf_op | source)
XLA Modules:
  0.0 230.9 jit_solution(13776051326965152967)
XLA Ops:
  0.7 101.1 %shard_map.305 = (bf16[2048,1536]{1,0:T(8,128)(2,1)}, bf16[4,2,256,1536]{3,2,1,0:T(8,128)(2,1)}, bf16[4,8,48,384]{3,2,1,0:T(8,128)(2,1)}, bf16[4,8,48,384]{3,2,1...) custom-call(bf16[256,1536]{1,0:T(8,128)(2,1)} %tok.3, ...), custom_call_target="tpu_custom_call" | custom-call | tf_op jit(solution)/shard_map/pallas_call | solution.py:1168
  101.8 20.5 %shard_map.306 = (bf16[4,2,256,1536]{3,2,1,0:T(8,128)(2,1)}, bf16[2048,384]{1,0:T(8,128)(2,1)}, bf16[2048,384]{1,0:T(8,128)(2,1)}, bf16[384,1536]{1,0:T(8,128)(2...) custom-call(f32[8,128]{1,0:T(8,128)} %get-tuple-element.58.lens, f32[8,512]{1,0:T(8,128)} %get-tuple-element.59.stats, ...), custom_call_target="tpu_custom_call" | custom-call | tf_op jit(solution)/shard_map/pallas_call | solution.py:1246
  122.3 0.0 copy-start.1
  122.3 0.0 copy-start.5
  122.3 0.0 copy-start.6
  122.3 0.0 copy-start.2
  122.4 0.0 copy-start.7
  122.4 0.0 copy-start.8
  122.4 0.0 copy-start
  122.4 0.0 copy-start.3
  122.4 0.0 copy-start.4
  122.4 91.8 %shard_map.307 = (bf16[4,96,1536]{2,1,0:T(8,128)(2,1)}, bf16[8,48,384]{2,1,0:T(8,128)(2,1)}, bf16[8,48,384]{2,1,0:T(8,128)(2,1)}, f32[48,384]{1,0:T(8,128)}, f32...) custom-call(f32[8,128]{1,0:T(8,128)} %get-tuple-element.58.lens, bf16[4,8,48,384]{3,2,1,0:T(8,128)(2,1)} %bitcast.31, ...), custom_call_target="tpu_custom_call" | custom-call | tf_op jit(solution)/shard_map/pallas_call | solution.py:1696
  214.2 0.8 fusion.8
  215.0 0.1 reshape.109
  215.1 0.1 reduce_sum.29
  215.1 0.1 concatenate.17
  215.2 0.8 slice.22
  216.0 0.1 concatenate.16
  216.1 0.1 reshape.110
  216.2 0.0 copy-done.1
  216.2 0.0 copy-done.5
  216.2 0.0 copy-done.6
  216.2 0.6 multiply_subtract_fusion.1
  216.8 0.1 reshape_reshape.10
  216.9 0.1 reshape_reshape.11
  217.0 0.9 slice_reduce_fusion
  217.9 0.0 copy-done.2
  217.9 0.0 copy-done.7
  217.9 0.0 copy-done.8
  217.9 0.7 multiply_subtract_fusion.2
  218.6 0.9 slice.18
  219.5 0.1 reshape_reshape.9
  219.6 0.1 reshape.106
  219.8 0.9 slice_reduce_fusion.1
  220.7 0.0 copy-done
  220.7 0.0 copy-done.3
  220.7 0.0 copy-done.4
  220.7 0.7 multiply_subtract_fusion
  221.4 9.3 %shard_map.308 = (bf16[256,1536]{1,0:T(8,128)(2,1)}, f32[256,1536]{1,0:T(8,128)}, f32[48,6448]{1,0:T(8,128)}, f32[48,6448]{1,0:T(8,128)}, f32[48,6448]{1,0:T(8,1...) custom-call(f32[8,128]{1,0:T(8,128)} %get-tuple-element.58.lens, bf16[256,1536]{1,0:T(8,128)(2,1)} %tok.3, ...), custom_call_target="tpu_custom_call" | custom-call | tf_op jit(solution)/shard_map/pallas_call | solution.py:1763
  (6 shorter events, 0.1 us)
Async XLA Ops:
  122.3 93.9 %copy-start.1 = (f32[3,48]{1,0:T(4,128)S(1)}, f32[3,48]{1,0:T(4,128)}, u32[]{:S(2)}) copy-start(f32[3,48]{1,0:T(4,128)} %head_params.1) | copy-start | bytes 1732
  122.3 93.9 %copy-start.5 = (f32[3,48]{1,0:T(4,128)S(1)}, f32[3,48]{1,0:T(4,128)}, u32[]{:S(2)}) copy-start(f32[3,48]{1,0:T(4,128)} %param.34) | copy-start | bytes 1732
  122.3 93.9 %copy-start.6 = (f32[3,48]{1,0:T(4,128)S(1)}, f32[3,48]{1,0:T(4,128)}, u32[]{:S(2)}) copy-start(f32[3,48]{1,0:T(4,128)} %param.35) | copy-start | bytes 1732
  122.3 95.5 %copy-start.2 = (f32[144]{0:T(256)S(1)}, f32[144]{0:T(256)}, u32[]{:S(2)}) copy-start(f32[144]{0:T(256)} %param.30) | copy-start | bytes 1732
  122.4 95.5 %copy-start.7 = (f32[144]{0:T(256)S(1)}, f32[144]{0:T(256)}, u32[]{:S(2)}) copy-start(f32[144]{0:T(256)} %param.31) | copy-start | bytes 1732
  122.4 95.5 %copy-start.8 = (f32[144]{0:T(256)S(1)}, f32[144]{0:T(256)}, u32[]{:S(2)}) copy-start(f32[144]{0:T(256)} %param.32) | copy-start | bytes 1732
  122.4 98.3 %copy-start = (f32[5,104]{1,0:T(8,128)S(1)}, f32[5,104]{1,0:T(8,128)}, u32[]{:S(2)}) copy-start(f32[5,104]{1,0:T(8,128)} %conv_w.1) | copy-start | bytes 6244
  122.4 98.3 %copy-start.3 = (f32[5,104]{1,0:T(8,128)S(1)}, f32[5,104]{1,0:T(8,128)}, u32[]{:S(2)}) copy-start(f32[5,104]{1,0:T(8,128)} %param.28) | copy-start | bytes 6244
  122.4 98.3 %copy-start.4 = (f32[5,104]{1,0:T(8,128)S(1)}, f32[5,104]{1,0:T(8,128)}, u32[]{:S(2)}) copy-start(f32[5,104]{1,0:T(8,128)} %param.29) | copy-start | bytes 6244
where the time goes:
time: 231 us
  Pallas kernels  223 us (97%)
  other arithmetic  3.85 us (2%)
  local copies, waits for them, and re-layouts  3.3 us (1%)
    pallas_call x1, Pallas kernels, run_fore(): pl.pallas_call(fore_kernel, in_specs=[ANY, ANY] + [whole] * 6, out_specs=...  101 us
    pallas_call x1, Pallas kernels, run_back(): pl.pallas_call(back_kernel, grid=(QUADS,), in_specs=[full_spec(lens.shape...  91.8 us
    pallas_call x1, Pallas kernels, run_gate(): pl.pallas_call(gate_kernel, grid=(QUADS,), in_specs=[full_spec(a.shape) f...  20.5 us
    pallas_call x1, Pallas kernels, run_finish(): pl.pallas_call(finish_kernel, in_specs=[whole] * len(args), out_specs=[wh...  9.28 us

commit v1 on v0

--- a/solution.py
+++ b/solution.py
@@ -1508,11 +1508,10 @@
         def free():
             swaps[1][k + 2].wait_send()
 
+    grad_all = jnp.concatenate([dgate[...], grad_x, grad_com], axis=1)
+    w_all = jnp.concatenate([w_gate[...], w_x[...], w_com[...]], axis=1)
     for side in range(2):
-        rows = slice(side * BLOCK, (side + 1) * BLOCK)
-        en_part[slot % 2, side] = low16(
-            mm_t(dgate[rows], w_gate[...]) + mm_t(grad_x[rows], w_x[...]) + mm_t(grad_com[rows], w_com[...])
-        )
+        en_part[slot % 2, side] = low16(mm_t(grad_all[side * BLOCK : (side + 1) * BLOCK], w_all))
     for k in range(QUADS):
 
         @pl.when(slot == k)
@@ -1715,87 +1714,97 @@
     )(lens, gate_grads, out_grads, branch, *fixed, *grouped)
 
 
-def adam_refs(refs, index, gradient, rate):
+def adam_refs(refs, columns, gradient, rate):
     weight, first, second, weight_new, first_new, second_new = refs
-    results = adam_update(weight[index], first[index], second[index], gradient, rate)
+    results = adam_update(weight[:, columns], first[:, columns], second[:, columns], gradient, rate)
     for ref, value in zip((weight_new, first_new, second_new), results):
-        ref[index] = value
+        ref[:, columns] = value
+
+
+RUNS = 2 * PLANES
+PIECE = 2 * OWN
+STEPS = 3
+RUNS_STEP = 3
 
 
 def finish_kernel(
-    lens, tok, cot, sum_branch, grad_rows, r_out, all_gate, all_x, sum_com,
+    lens, all_gate, all_x, sum_com, tok, cot, sum_branch, grad_rows, r_out,
     in_w, in_m, in_v, out_w, out_m, out_v,
     mixed_out, grad_input, in_wn, in_mn, in_vn, out_wn, out_mn, out_vn
 ):
     f32 = jnp.float32
+    step = pl.program_id(0)
     core = lax.axis_index("seq")
-    position = (iota((BLOCK, 1), 0) + core * BLOCK).astype(f32)
-    live = (position < lens[0:1, 0:1]).astype(f32)
-    mixed_out[...] = (tok[...].astype(f32) + live * sum_branch[...]).astype(jnp.bfloat16)
-    grad_input[...] = cot[...].astype(f32) + grad_rows[...]
     ins = (in_w, in_m, in_v, in_wn, in_mn, in_vn)
     rows = in_w.shape[0]
     lanes = iota((rows, LANES), 1)
+
+    @pl.when(step < 2)
+    def positions():
+        count = tok.shape[0]
+        position = (iota((count, 1), 0) + core * BLOCK + step * count).astype(f32)
+        live = (position < lens[0:1, 0:1]).astype(f32)
+        mixed_out[...] = (tok[...].astype(f32) + live * sum_branch[...]).astype(jnp.bfloat16)
+        grad_input[...] = cot[...].astype(f32) + grad_rows[...]
+
+    total = r_out[0].astype(f32) + r_out[1].astype(f32) + r_out[2].astype(f32) + r_out[3].astype(f32)
+    adam_refs((out_w, out_m, out_v, out_wn, out_mn, out_vn), slice(None), total, rate_out)
+
     for part, source in ((0, all_gate), (1, all_x)):
         for run in range(PLANES):
-            side, near = divmod(run, 2)
-            tiles = []
-            for t in range(2 * PAIRS):
-                halves = []
-                for b in range(2):
-                    p, i = divmod(2 * t + b, 3)
-                    index = 3 * near + i
-                    tile = source[2 * p + side, :, (index // 2) * LANES : (index // 2 + 1) * LANES].astype(f32)
-                    halves.append(tile if index % 2 == b else pltpu.roll(tile, HDIM, 1))
-                tiles.append(jnp.where(lanes < HDIM, halves[0], halves[1]))
-            start = part * DIN + run * 2 * OWN
-            adam_refs(ins, (slice(None), slice(start, start + 2 * OWN)), jnp.concatenate(tiles, axis=1), rate_in)
-    adam_refs(ins, (slice(None), slice(2 * DIN, 2 * DIN + COMMON)), sum_com[:, :COMMON], rate_in)
-    total = r_out[0].astype(f32) + r_out[1].astype(f32) + r_out[2].astype(f32) + r_out[3].astype(f32)
-    adam_refs((out_w, out_m, out_v, out_wn, out_mn, out_vn), (slice(None), slice(None)), total, rate_out)
-
-
-def run_finish(*args):
-    tok, cot, in_w, out_w = (args[1], args[2], args[9], args[12])
-    shapes = [(tok.shape, jnp.bfloat16), (cot.shape, jnp.float32)]
-    shapes += [(in_w.shape, jnp.float32)] * 3 + [(out_w.shape, jnp.float32)] * 3
-    whole = pl.BlockSpec(memory_space=pltpu.VMEM)
+
+            place_at = PLANES * part + run
+            start = place_at % RUNS_STEP * PIECE
+
+            @pl.when(step == place_at // RUNS_STEP)
+            def in_columns():
+                side, near = divmod(run, 2)
+                for t in range(2 * PAIRS):
+                    halves = []
+                    for b in range(2):
+                        p, i = divmod(2 * t + b, RUN_HALVES)
+                        index = RUN_HALVES * near + i
+                        tile = source[2 * p + side, :, (index // 2) * LANES : (index // 2 + 1) * LANES].astype(f32)
+                        halves.append(tile if index % 2 == b else pltpu.roll(tile, HDIM, 1))
+                    gradient = jnp.where(lanes < HDIM, halves[0], halves[1])
+                    adam_refs(ins, slice(start + t * LANES, start + (t + 1) * LANES), gradient, rate_in)
+
+    @pl.when(step == RUNS // RUNS_STEP)
+    def common_columns():
+        start = RUNS % RUNS_STEP * PIECE
+        adam_refs(ins, slice(start, start + COMMON_PAD), sum_com[...], rate_in)
+
+
+def run_finish(lens, tok, cot, sum_branch, grad_rows, r_out, all_gate, all_x, sum_com, *weights):
+    in_w, out_w = (weights[0], weights[3])
+    f32 = jnp.float32
+    rows = BLOCK // 2
+    out_rows = out_w.shape[0] // STEPS
+
+    def positions():
+        return pl.BlockSpec((rows, D), lambda s: (jnp.minimum(s, 1), 0))
+
+    def in_block():
+        return pl.BlockSpec((in_w.shape[0], RUNS_STEP * PIECE), lambda s: (0, s))
+
+    def out_block():
+        return pl.BlockSpec((out_rows, D), lambda s: (s, 0))
+
+    shapes = [(tok.shape, jnp.bfloat16), (cot.shape, f32)] + [(in_w.shape, f32)] * 3 + [(out_w.shape, f32)] * 3
     return pl.pallas_call(
         finish_kernel,
-        in_specs=[whole] * len(args),
-        out_specs=[whole] * len(shapes),
+        grid=(STEPS,),
+        in_specs=[full_spec(a.shape) for a in (lens, all_gate, all_x, sum_com)]
+        + [positions() for unused in range(4)]
+        + [pl.BlockSpec((PLANES, out_rows, D), lambda s: (0, s, 0))]
+        + [in_block() for unused in range(3)]
+        + [out_block() for unused in range(3)],
+        out_specs=[positions(), positions()]
+        + [in_block() for unused in range(3)]
+        + [out_block() for unused in range(3)],
         out_shape=[jax.ShapeDtypeStruct(s, kind) for s, kind in shapes],
         compiler_params=pltpu.CompilerParams(vmem_limit_bytes=VMEM_GRANT),
-    )(*args)
-
-
-def pick_runs(array, plane_runs, quad, core):
-    lead = array.shape[:-1]
-    width = array.shape[-1] // (PLANES * QUADS)
-    split = array.reshape(lead + (2, 2, QUADS, width))
-    zero = 0
-    n = len(lead)
-    taken = lax.dynamic_slice(
-        split, (zero,) * n + (core, 0, quad, 0), lead + (1, 2, 1, width)
-    )
-    return taken.reshape(lead + (2 * width,))
-
-
-def put_runs(array, quad, core):
-    lead = array.shape[:-1]
-    width = array.shape[-1] // 2
-    zeros = jnp.zeros(lead + (2, 2, QUADS, width), array.dtype)
-    n = len(lead)
-    full = lax.dynamic_update_slice(
-        zeros, array.reshape(lead + (1, 2, 1, width)), (0,) * n + (core, 0, quad, 0)
-    )
-    return full.reshape(lead + (width * PLANES * QUADS,))
-
-
-def rank_slices(array):
-    rows = array.shape[0]
-    split = array.reshape(rows, 2, 2, QUADS, RUN)
-    return split.transpose(3, 1, 0, 2, 4).reshape(RANKS, rows, OWN)
+    )(lens, all_gate, all_x, sum_com, tok, cot, sum_branch, grad_rows, r_out, *weights)
 
 
 def rank_join(array):

time: 231 us -> 231 us (level)
  no operation moved by 1% of the time
where the time goes in v1:
time: 231 us; the launch traced here: 230 us
  Pallas kernels  222 us (96%)
  other arithmetic  3.85 us (2%)
  local copies, waits for them, and re-layouts  3.3 us (1%)
    pallas_call x1, Pallas kernels, run_fore(): pl.pallas_call(fore_kernel, in_specs=[ANY, ANY] + [whole] * 6, out_specs=...  101 us
    pallas_call x1, Pallas kernels, run_back(): pl.pallas_call(back_kernel, grid=(QUADS,), in_specs=[full_spec(lens.shape...  91.5 us
    pallas_call x1, Pallas kernels, run_gate(): pl.pallas_call(gate_kernel, grid=(QUADS,), in_specs=[full_spec(a.shape) f...  20.5 us
    pallas_call x1, Pallas kernels, run_finish(): pl.pallas_call(finish_kernel, grid=(STEPS,), in_specs=[full_spec(a.shape)...  8.86 us

profile of v1, /device:TPU:0, one launch (start us, length us, event | category | flops | bytes accessed | tf_op | source)
XLA Modules:
  0.0 230.2 jit_solution(14676734582919752462)
XLA Ops:
  0.7 101.1 %shard_map.305 = (bf16[2048,1536]{1,0:T(8,128)(2,1)}, bf16[4,2,256,1536]{3,2,1,0:T(8,128)(2,1)}, bf16[4,8,48,384]{3,2,1,0:T(8,128)(2,1)}, bf16[4,8,48,384]{3,2,1...) custom-call(bf16[256,1536]{1,0:T(8,128)(2,1)} %tok.3, ...), custom_call_target="tpu_custom_call" | custom-call | tf_op jit(solution)/shard_map/pallas_call | solution.py:1168
  101.8 20.5 %shard_map.306 = (bf16[4,2,256,1536]{3,2,1,0:T(8,128)(2,1)}, bf16[2048,384]{1,0:T(8,128)(2,1)}, bf16[2048,384]{1,0:T(8,128)(2,1)}, bf16[384,1536]{1,0:T(8,128)(2...) custom-call(f32[8,128]{1,0:T(8,128)} %get-tuple-element.58.lens, f32[8,512]{1,0:T(8,128)} %get-tuple-element.59.stats, ...), custom_call_target="tpu_custom_call" | custom-call | tf_op jit(solution)/shard_map/pallas_call | solution.py:1246
  122.3 0.0 copy-start.1
  122.3 0.0 copy-start.5
  122.3 0.0 copy-start.6
  122.3 0.0 copy-start.2
  122.4 0.0 copy-start.7
  122.4 0.0 copy-start.8
  122.4 0.0 copy-start
  122.4 0.0 copy-start.3
  122.4 0.0 copy-start.4
  122.4 91.5 %shard_map.307 = (bf16[4,96,1536]{2,1,0:T(8,128)(2,1)}, bf16[8,48,384]{2,1,0:T(8,128)(2,1)}, bf16[8,48,384]{2,1,0:T(8,128)(2,1)}, f32[48,384]{1,0:T(8,128)}, f32...) custom-call(f32[8,128]{1,0:T(8,128)} %get-tuple-element.58.lens, bf16[4,8,48,384]{3,2,1,0:T(8,128)(2,1)} %bitcast.31, ...), custom_call_target="tpu_custom_call" | custom-call | tf_op jit(solution)/shard_map/pallas_call | solution.py:1695
  213.9 0.8 fusion.8
  214.7 0.1 reshape.109
  214.8 0.1 reduce_sum.29
  214.9 0.1 concatenate.17
  215.0 0.8 slice.22
  215.8 0.1 concatenate.16
  215.9 0.1 reshape.110
  216.0 0.0 copy-done.1
  216.0 0.0 copy-done.5
  216.0 0.0 copy-done.6
  216.0 0.6 multiply_subtract_fusion.1
  216.6 0.1 reshape_reshape.10
  216.7 0.1 reshape_reshape.11
  216.8 0.9 slice_reduce_fusion
  217.6 0.0 copy-done.2
  217.6 0.0 copy-done.7
  217.7 0.0 copy-done.8
  217.7 0.7 multiply_subtract_fusion.2
  218.3 0.9 slice.18
  219.2 0.1 reshape_reshape.9
  219.4 0.1 reshape.106
  219.5 0.9 slice_reduce_fusion.1
  220.4 0.0 copy-done
  220.5 0.0 copy-done.3
  220.5 0.0 copy-done.4
  220.5 0.7 multiply_subtract_fusion
  221.2 8.9 %shard_map.308 = (bf16[256,1536]{1,0:T(8,128)(2,1)}, f32[256,1536]{1,0:T(8,128)}, f32[48,6448]{1,0:T(8,128)}, f32[48,6448]{1,0:T(8,128)}, f32[48,6448]{1,0:T(8,1...) custom-call(f32[8,128]{1,0:T(8,128)} %get-tuple-element.58.lens, ...), custom_call_target="tpu_custom_call" | custom-call | tf_op jit(solution)/shard_map/pallas_call | solution.py:1794
  (6 shorter events, 0.1 us)
Async XLA Ops:
  122.3 93.7 %copy-start.1 = (f32[3,48]{1,0:T(4,128)S(1)}, f32[3,48]{1,0:T(4,128)}, u32[]{:S(2)}) copy-start(f32[3,48]{1,0:T(4,128)} %head_params.1) | copy-start | bytes 1732
  122.3 93.7 %copy-start.5 = (f32[3,48]{1,0:T(4,128)S(1)}, f32[3,48]{1,0:T(4,128)}, u32[]{:S(2)}) copy-start(f32[3,48]{1,0:T(4,128)} %param.34) | copy-start | bytes 1732
  122.3 93.7 %copy-start.6 = (f32[3,48]{1,0:T(4,128)S(1)}, f32[3,48]{1,0:T(4,128)}, u32[]{:S(2)}) copy-start(f32[3,48]{1,0:T(4,128)} %param.35) | copy-start | bytes 1732
  122.3 95.3 %copy-start.2 = (f32[144]{0:T(256)S(1)}, f32[144]{0:T(256)}, u32[]{:S(2)}) copy-start(f32[144]{0:T(256)} %param.30) | copy-start | bytes 1732
  122.4 95.3 %copy-start.7 = (f32[144]{0:T(256)S(1)}, f32[144]{0:T(256)}, u32[]{:S(2)}) copy-start(f32[144]{0:T(256)} %param.31) | copy-start | bytes 1732
  122.4 95.3 %copy-start.8 = (f32[144]{0:T(256)S(1)}, f32[144]{0:T(256)}, u32[]{:S(2)}) copy-start(f32[144]{0:T(256)} %param.32) | copy-start | bytes 1732
  122.4 98.1 %copy-start = (f32[5,104]{1,0:T(8,128)S(1)}, f32[5,104]{1,0:T(8,128)}, u32[]{:S(2)}) copy-start(f32[5,104]{1,0:T(8,128)} %conv_w.1) | copy-start | bytes 6244
  122.4 98.1 %copy-start.3 = (f32[5,104]{1,0:T(8,128)S(1)}, f32[5,104]{1,0:T(8,128)}, u32[]{:S(2)}) copy-start(f32[5,104]{1,0:T(8,128)} %param.28) | copy-start | bytes 6244
  122.4 98.1 %copy-start.4 = (f32[5,104]{1,0:T(8,128)S(1)}, f32[5,104]{1,0:T(8,128)}, u32[]{:S(2)}) copy-start(f32[5,104]{1,0:T(8,128)} %param.29) | copy-start | bytes 6244
